TPU v7x, 128 devices: a whole 4x4x4 slice. The times are simulated.
128 devices in a mesh: group: 64 (over z, y, x), local: 2 (over core).
Axes of the slice: x: 4, y: 4, z: 4, core: 2. Of those that a mesh axis runs over, the one named last changes fastest.
Arguments:
- tokens: bfloat16 [65536, 2048], P(('group', 'local')), may hold values from -6 to 6
- cotangent: bfloat16 [65536, 2048], P(('group', 'local')), may hold values from -6 to 6
- row_slot: int32 [65536], P(('group', 'local')), may hold values from 0 to 1
- placement: int32 [64, 2], replicated, may hold values from 0 to 7, as said below
- master: float32 [8, 3, 384, 2048], P(None, None, 'group', 'local'), may hold values from -0.125 to 0.125
- first_moment: float32 [8, 3, 384, 2048], P(None, None, 'group', 'local'), may hold values from -2 to 2
- second_moment: float32 [8, 3, 384, 2048], P(None, None, 'group', 'local'), may hold values from 1 to 1000
Outputs:
- layer_out: bfloat16 [65536, 2048], P(('group', 'local'))
- input_grad: bfloat16 [65536, 2048], P(('group', 'local'))
- new_master: float32 [8, 3, 384, 2048], P(None, None, 'group', 'local')
- new_first: float32 [8, 3, 384, 2048], P(None, None, 'group', 'local')
- new_second: float32 [8, 3, 384, 2048], P(None, None, 'group', 'local')
Inputs may be any that keep to these rules, and one draw needn't show every extreme that they name: `placement`: the 2 slots of a group name different experts; every expert is named by at least one slot.
All inputs are finite; a program needn't handle non-finite values.
Results may differ from a plain program's by a relative error of at most 0.0071.
Values may be sent and summed in bfloat16 or wider, within the bound.
No kernel may reach another device: no remote copies, remote signals or barrier semaphores. Data moves between devices by JAX's collectives and lax.ppermute only.
A program may use at most 128 MiB of HBM per device.

v0:
```python
import functools
import jax
import jax.numpy as jnp
import numpy as np
from jax import lax
from jax.experimental import pallas as pl
from jax.experimental.pallas import tpu as pltpu
from jax.sharding import PartitionSpec as P

loss_scale = 4.0
beta_first = 0.9
beta_second = 0.95
learn_rate = 0.001
adam_epsilon = 1e-08
bias_first = 1.0 - 0.9**10
bias_second = 1.0 - 0.95**10

SIDE = 4
CHAINS = 3
BOTH = ("group", "local")
SHIFTS = (4, 2, 0)
AXES = ((2, 1, 0), (1, 0, 2), (0, 2, 1))


def place(coords, core):
    return ((coords[0] * SIDE + coords[1]) * SIDE + coords[2]) * 2 + core


def step_pairs(axis, offsets):
    pairs = []
    for group in range(SIDE**3):
        for core in range(2):
            coords = [group // 16, group // 4 % 4, group % 4]
            here = place(coords, core)
            coords[axis] ^= offsets[core]
            pairs.append((here, place(coords, core)))
    return pairs


CORE_PAIRS = [(i, i ^ 1) for i in range(2 * SIDE**3)]
ONE, BACK, ACROSS = (1, 3), (3, 1), (2, 2)
STEPS = ((0, 0), ONE, BACK, ACROSS)


def hop(value, axis, offsets):
    return lax.ppermute(value, BOTH, step_pairs(axis, offsets))


def swap(value):
    return lax.ppermute(value, BOTH, CORE_PAIRS)


def together(*values):
    return lax.optimization_barrier(values)


def contract_last(left, right):
    return lax.dot_general(
        left, right, (((1,), (1,)), ((), ())), preferred_element_type=jnp.float32
    )


def contract_first(left, right):
    return lax.dot_general(
        left, right, (((0,), (0,)), ((), ())), preferred_element_type=jnp.float32
    )


def matmul(left, right):
    return jnp.dot(left, right, preferred_element_type=jnp.float32)


VMEM = pl.BlockSpec(memory_space=pltpu.VMEM)
SMEM = pl.BlockSpec(memory_space=pltpu.SMEM)
LIMIT = pltpu.CompilerParams(vmem_limit_bytes=16 * 1024 * 1024)


def shape_of(*dims):
    return jax.ShapeDtypeStruct(dims, jnp.bfloat16)


def spots(core):
    return (0, 1 + core, 2 - core, 3)


def weave_kernel(table_ref, own, one, rest, out, turned):
    first = table_ref[8] == 0
    for m in range(3):
        for r in range(2):
            near = one[m, r].astype(jnp.float32)
            back = rest[0, m, r].astype(jnp.float32)
            turned[m, :, r] = own[m, r].astype(jnp.float32)
            turned[m, :, 2 + r] = jnp.where(first, near, back)
            turned[m, :, 4 + r] = jnp.where(first, back, near)
            turned[m, :, 6 + r] = rest[1, m, r].astype(jnp.float32)
    out[...] = turned[...].astype(jnp.bfloat16)


def weave(table, own, one, rest):
    _, _, experts, columns = own.shape
    return pl.pallas_call(
        weave_kernel,
        out_shape=shape_of(3, experts, 8, columns),
        in_specs=[SMEM] + [VMEM] * 3,
        out_specs=VMEM,
        scratch_shapes=[pltpu.VMEM((3, experts, 8, columns), jnp.float32)],
        compiler_params=LIMIT,
        name="weave",
    )(table, own, one, rest)


def unweave_kernel(table_ref, own, came, last, out, one, rest, turned):
    first = table_ref[8] == 0
    turned[...] = (
        own[...].astype(jnp.float32) + came[0].astype(jnp.float32) + last[...].astype(jnp.float32)
    )
    for m in range(3):
        for r in range(2):
            left = turned[m, :, 2 + r]
            right = turned[m, :, 4 + r]
            out[m, r] = turned[m, :, r]
            one[m, r] = jnp.where(first, left, right).astype(jnp.bfloat16)
            rest[0, m, r] = jnp.where(first, right, left).astype(jnp.bfloat16)
            rest[1, m, r] = turned[m, :, 6 + r].astype(jnp.bfloat16)


def unweave(table, own, came, last):
    _, experts, _, columns = own.shape
    return pl.pallas_call(
        unweave_kernel,
        out_shape=[
            jax.ShapeDtypeStruct((3, 2, experts, columns), jnp.float32),
            shape_of(3, 2, experts, columns),
            shape_of(2, 3, 2, experts, columns),
        ],
        in_specs=[SMEM] + [VMEM] * 3,
        out_specs=[VMEM] * 3,
        scratch_shapes=[pltpu.VMEM((3, experts, 8, columns), jnp.float32)],
        compiler_params=LIMIT,
        name="unweave",
    )(table, own, came, last)


def pick_kernel(table_ref, p0, p1, p2, p3, *outs):
    spot = spots(table_ref[8])
    for index, out in enumerate(outs):
        for k in range(2):
            e = table_ref[2 * index + k]
            for b, p in enumerate((p0, p1, p2, p3)):
                out[k, :, spot[b]] = p[:, e]


def pick(table, plane):
    columns = plane[0].shape[-1]
    return pl.pallas_call(
        pick_kernel,
        out_shape=[shape_of(2, 3, 4, 8, columns)] * 4,
        in_specs=[SMEM] + [VMEM] * 4,
        out_specs=[VMEM] * 4,
        compiler_params=LIMIT,
        name="pick",
    )(table, *plane)


def first_kernel(table_ref, tok0, tok1, cot0, cot1, mask, a0, a1, a2, a3, sums, weights):
    core = table_ref[8]
    columns = a0.shape[-1]
    rows = tok0.shape[0]
    step = 256
    for spot, a in zip(spots(core), (a0, a1, a2, a3)):
        weights[:, :, spot] = a[...]
    half = pl.ds(pl.multiple_of(core * columns, columns), columns)
    w = [
        (weights[k, 0:2].reshape(256, columns), weights[k, 2].reshape(128, columns))
        for k in range(2)
    ]
    for b, (tok, cot) in enumerate(((tok0, cot0), (tok1, cot1))):
        for r in range(0, rows, step):
            here = slice(r, r + step)
            there = slice(rows * b + r, rows * b + r + step)
            chosen = mask[there] > 0.0
            tok_part = tok[here, half]
            cot_part = cot[here, half]
            pre = [contract_last(tok_part, w[k][0]) for k in range(2)]
            d_hidden = [contract_last(cot_part, w[k][1]) for k in range(2)]
            sums[0, there] = jnp.where(chosen, pre[0][:, :128], pre[1][:, :128])
            sums[1, there] = jnp.where(chosen, pre[0][:, 128:], pre[1][:, 128:])
            sums[2, there] = jnp.where(chosen, d_hidden[0], d_hidden[1])


def first(table, rows_in, mask, arrived):
    columns = arrived[0].shape[-1]
    rows = mask.shape[0]
    return pl.pallas_call(
        first_kernel,
        out_shape=[
            jax.ShapeDtypeStruct((3, rows, 128), jnp.float32),
            shape_of(2, 3, 4, 32, columns),
        ],
        in_specs=[SMEM] + [VMEM] * 9,
        out_specs=[VMEM] * 2,
        compiler_params=pltpu.CompilerParams(vmem_limit_bytes=24 * 1024 * 1024),
        name="first",
    )(table, *rows_in, mask, *arrived)


def second_kernel(
    table_ref, tok0, tok1, cot0, cot1, mask, sums, got, o0, o1, o2, o3, hidden, pair, turned
):
    core = table_ref[8]
    columns = o0.shape[-1]
    rows = tok0.shape[0]
    step = 256
    for r in range(0, 2 * rows, step):
        here = slice(r, r + step)
        there = slice((r + rows) % (2 * rows), (r + rows) % (2 * rows) + step)
        gate_pre = sums[0, here] + got[0, there]
        up_pre = sums[1, here] + got[1, there]
        d_hidden = sums[2, here] + got[2, there]
        sigmoid_gate = jax.nn.sigmoid(gate_pre)
        act = gate_pre * sigmoid_gate
        d_gate = d_hidden * up_pre * sigmoid_gate * (1.0 + gate_pre * (1.0 - sigmoid_gate))
        three = (d_gate, d_hidden * act, act * up_pre)
        chosen = mask[here] > 0.0
        for k in range(2):
            for m in range(3):
                part = jnp.where(chosen, three[m], 0.0) if k == 0 else jnp.where(chosen, 0.0, three[m])
                part = part.astype(jnp.bfloat16)
                if m < 2:
                    pair[here, 256 * k + 128 * m : 256 * k + 128 * m + 128] = part
                else:
                    hidden[here, 128 * k : 128 * k + 128] = part
                line = 256 * k + 128 * m if m < 2 else 512 + 128 * k
                turned[line : line + 128, here] = part.T
    start = pl.multiple_of(core * columns, columns)
    swapped = core == 1
    for c in range(0, columns, step):
        cols = pl.ds(start + c, step)
        out_cols = slice(c, c + step)
        both = matmul(turned[:512, :rows], tok0[:, cols]) + matmul(turned[:512, rows:], tok1[:, cols])
        down = matmul(turned[512:, :rows], cot0[:, cols]) + matmul(turned[512:, rows:], cot1[:, cols])
        for k in range(2):
            for m in range(3):
                line = both[256 * k + 128 * m :][:128] if m < 2 else down[128 * k :][:128]
                line = line.astype(jnp.bfloat16)
                q = [line[32 * i : 32 * i + 32] for i in range(4)]
                o0[k, m, :, out_cols] = q[0]
                o1[k, m, :, out_cols] = jnp.where(swapped, q[2], q[1])
                o2[k, m, :, out_cols] = jnp.where(swapped, q[1], q[2])
                o3[k, m, :, out_cols] = q[3]


def second(table, rows_in, mask, sums, got, columns):
    rows = mask.shape[0]
    return pl.pallas_call(
        second_kernel,
        out_shape=[shape_of(2, 3, 32, columns)] * 4 + [shape_of(rows, 256), shape_of(rows, 512)],
        in_specs=[SMEM] + [VMEM] * 7,
        out_specs=[VMEM] * 6,
        scratch_shapes=[pltpu.VMEM((768, rows), jnp.bfloat16)],
        compiler_params=pltpu.CompilerParams(vmem_limit_bytes=24 * 1024 * 1024),
        name="second",
    )(table, *rows_in, mask, sums, got)


def rows_kernel(start, table_ref, *refs):
    hidden, pair, weights = refs[0:3], refs[3:6], refs[6:9]
    added, (layer_out, grad_out) = refs[9:-2], refs[-2:]
    columns = weights[0].shape[-1]
    rows = slice(start, start + layer_out.shape[0])
    step = 512
    if added:
        core = table_ref[8]
        near = pl.multiple_of(core * columns, columns)
        far = pl.ds(pl.multiple_of((1 - core) * columns, columns), columns)
        layer_out[:, far] = added[0][...]
        grad_out[:, far] = added[1][...]
    for c in range(0, columns, step):
        part = slice(c, c + step)
        cols = pl.ds(near + c, step) if added else part
        layer = 0.0
        grad = 0.0
        for chain in range(CHAINS):
            w = weights[chain]
            down = jnp.concatenate([w[k, 2, :, :, part].reshape(128, step) for k in range(2)], 0)
            layer = layer + matmul(hidden[chain][rows], down)
            for k in range(2):
                both = w[k, 0:2, :, :, part].reshape(256, step)
                grad = grad + matmul(pair[chain][rows, 256 * k : 256 * k + 256], both)
        layer_out[:, cols] = layer.astype(jnp.bfloat16)
        grad_out[:, cols] = grad.astype(jnp.bfloat16)


def rows_out(table, start, hidden, pair, weights, added):
    columns = weights[0].shape[-1]
    rows = hidden[0].shape[0] // 2
    return pl.pallas_call(
        functools.partial(rows_kernel, start),
        out_shape=[shape_of(rows, 2 * columns if added else columns)] * 2,
        in_specs=[SMEM] + [VMEM] * (9 + len(added)),
        out_specs=[VMEM] * 2,
        compiler_params=pltpu.CompilerParams(vmem_limit_bytes=24 * 1024 * 1024),
        name="rows_out",
    )(table, *hidden, *pair, *weights, *added)


def merge_kernel(table_ref, c0, c1, c2, c3, own, one, rest, total):
    spot = spots(table_ref[8])
    total[...] = jnp.zeros_like(total)
    for index, came in enumerate((c0, c1, c2, c3)):
        for k in range(2):
            e = table_ref[2 * index + k]
            for p in range(4):
                total[p, :, e] += came[k, :, p].astype(jnp.float32)
    own[...] = total[0].astype(jnp.bfloat16)
    one[...] = total[spot[1]].astype(jnp.bfloat16)
    rest[0] = total[spot[2]].astype(jnp.bfloat16)
    rest[1] = total[3].astype(jnp.bfloat16)


def merge(table, came, experts):
    columns = came[0].shape[-1]
    return pl.pallas_call(
        merge_kernel,
        out_shape=[shape_of(*lead, 3, experts, 8, columns) for lead in ((), (), (2,))],
        in_specs=[SMEM] + [VMEM] * 4,
        out_specs=[VMEM] * 3,
        scratch_shapes=[pltpu.VMEM((4, 3, experts, 8, columns), jnp.float32)],
        compiler_params=LIMIT,
        name="merge",
    )(table, *[c.reshape(2, 3, 4, 8, columns) for c in came])


def shards(tokens, cotangent, row_slot, placement, master, first_moment, second_moment):
    group = lax.axis_index("group")
    core = lax.axis_index("local")
    experts = master.shape[0]
    columns = master.shape[3]
    rows = tokens.shape[0]

    steps = np.array(
        [[[step[c] << SHIFTS[axes[2]] for step in STEPS] for axes in AXES] for c in range(2)], np.int32
    ).reshape(2, -1)
    there = group ^ jnp.where(core == 0, jnp.asarray(steps[0]), jnp.asarray(steps[1]))
    seen = there[:, None] == jnp.arange(SIDE**3)[None]
    pairs = jnp.sum(jnp.where(seen[:, :, None], placement[None], 0), 1)
    pairs = pairs.reshape(CHAINS, 2 * SIDE)
    table = jnp.concatenate([pairs, jnp.full((CHAINS, 1), core)], 1)

    narrow = master.astype(jnp.bfloat16).transpose(1, 2, 0, 3)
    near = [axes[0] for axes in AXES]
    mid = [axes[1] for axes in AXES]
    last = [axes[2] for axes in AXES]
    each = range(CHAINS)
    blocks = [narrow[:, 2 * c : 2 * c + 2] for c in each]
    (ones,) = together([hop(blocks[c], near[c], ONE) for c in each])
    rests = [hop(jnp.stack([blocks[c], ones[c]], 0), near[c], BACK) for c in each]
    rows_in = [tokens, swap(tokens), cotangent, swap(cotangent)]
    slots = jnp.concatenate([row_slot, swap(row_slot)], 0)
    chosen = jnp.broadcast_to((slots == 0)[:, None], (2 * rows, 128)).astype(jnp.float32)
    rests, rows_in, chosen = together(rests, rows_in, chosen)
    (lines,) = together([weave(table[c], blocks[c], ones[c], rests[c]) for c in each])
    backs = [hop(lines[c], mid[c], BACK) for c in each]
    (ones,) = together([hop(lines[c], mid[c], ONE) for c in each])
    acrosses = [hop(ones[c], mid[c], BACK) for c in each]
    backs, acrosses = together(backs, acrosses)
    packed = [pick(table[c], [lines[c], ones[c], backs[c], acrosses[c]]) for c in each]
    (packed,) = together(packed)
    arrived = [
        [packed[c][0]] + [hop(p, last[c], s) for p, s in zip(packed[c][1:], STEPS[1:])] for c in each
    ]
    (arrived,) = together(arrived)

    sums = []
    weights = []
    for c in each:
        blocks = [a.reshape(2, 3, 32, columns) for a in arrived[c]]
        one_sums, one_weights = first(table[c], rows_in, chosen, blocks)
        sums.append(one_sums)
        weights.append(one_weights)
    got = [swap(v) for v in sums]
    sent = []
    hidden = []
    pair = []
    for c in each:
        *packed, one_hidden, one_pair = second(table[c], rows_in, chosen, sums[c], got[c], columns)
        sent.append(packed)
        hidden.append(one_hidden)
        pair.append(one_pair)

    merged = []
    for c in each:
        came = [sent[c][0]] + [hop(p, last[c], s) for p, s in zip(sent[c][1:], STEPS[1:])]
        merged.append(merge(table[c], came, experts))

    def add(one, came):
        return (one.astype(jnp.float32) + came[1].astype(jnp.float32)).astype(jnp.bfloat16)

    def scatter(parts, axes):
        (came,) = together([hop(parts[c][2], axes[c], BACK) for c in each])
        (ones,) = together([add(parts[c][1], came[c]) for c in each])
        (ones,) = together([hop(ones[c], axes[c], ONE) for c in each])
        return [(parts[c][0], came[c], ones[c]) for c in each]

    merged = scatter(merged, mid)
    sums = [unweave(table[c], *merged[c]) for c in each]

    far_rows = rows_out(table[0], rows, hidden, pair, weights, [])
    layer_out, input_grad = rows_out(
        table[0], 0, hidden, pair, weights, [swap(r) for r in far_rows]
    )
    sums, layer_out, input_grad = together(sums, layer_out, input_grad)
    parts = [
        own + came[0].astype(jnp.float32) + one.astype(jnp.float32)
        for own, came, one in scatter(sums, near)
    ]

    grads = jnp.concatenate(parts, 1).transpose(2, 0, 1, 3)
    scaled = grads / loss_scale
    new_first = beta_first * first_moment + (1.0 - beta_first) * scaled
    new_second = beta_second * second_moment + (1.0 - beta_second) * scaled * scaled
    new_master = master - learn_rate * (new_first / bias_first) / (
        jnp.sqrt(new_second / bias_second) + adam_epsilon
    )

    return layer_out, input_grad, new_master, new_first, new_second


def solution(mesh):
    state = P(None, None, "group", "local")
    rows = P(("group", "local"), None)
    return jax.shard_map(
        shards,
        mesh=mesh,
        in_specs=(rows, rows, P(("group", "local")), P(), state, state, state),
        out_specs=(rows, rows, state, state, state),
        check_vma=False,
    )
```

profile of v0, /device:TPU:1, one launch (start us, length us, event | category | flops | bytes accessed | tf_op | source)
XLA Modules:
  0.0 199.3 jit_solution(22144035963592993)
XLA Ops:
  0.7 1.5 collective-permute-start.6
  3.4 3.9 %collective-permute-start.2 = (bf16[3,2,8,1024]{3,2,1,0:T(8,128)(2,1)S(1)}, bf16[3,2,8,1024]{3,2,1,0:T(8,128)(2,1)S(1)}, u32[]{:S(2)}, u32[]{:S(2)}) collective-permute-start(bf16[3,2,8,1024]{3,2,1,0:T(8,128)(2,1)S(1)} %get-tuple-element.279.own), channel_id=1, source_target_pairs={{0,32},{1,97},{2,34},{3,99},{4,36},{5,101},{6,38},{7,103},{8,40},{... | collective-permute-start | bytes 294920 | tf_op jit(solution)/shard_map/ppermute | solution.py:46
  7.4 2.7 %collective-permute-start.1 = (bf16[3,2,8,1024]{3,2,1,0:T(8,128)(2,1)S(1)}, bf16[3,2,8,1024]{3,2,1,0:T(8,128)(2,1)S(1)}, u32[]{:S(2)}, u32[]{:S(2)}) collective-permute-start(bf16[3,2,8,1024]{3,2,1,0:T(8,128)(2,1)S(1)} %get-tuple-element.280.own), channel_id=1, source_target_pairs={{0,8},{1,25},{2,10},{3,27},{4,12},{5,29},{6,14},{7,31},{8,0},{9,17... | collective-permute-start | bytes 294920 | tf_op jit(solution)/shard_map/ppermute | solution.py:46
  10.1 2.5 %collective-permute-start = (bf16[3,2,8,1024]{3,2,1,0:T(8,128)(2,1)S(1)}, bf16[3,2,8,1024]{3,2,1,0:T(8,128)(2,1)S(1)}, u32[]{:S(2)}, u32[]{:S(2)}) collective-permute-start(bf16[3,2,8,1024]{3,2,1,0:T(8,128)(2,1)S(1)} %get-tuple-element.281.own), channel_id=1, source_target_pairs={{0,2},{1,7},{2,0},{3,5},{4,6},{5,3},{6,4},{7,1},{8,10},{9,15},{10,... | collective-permute-start | bytes 294920 | tf_op jit(solution)/shard_map/ppermute | solution.py:46
  13.1 1.6 collective-permute-done.one
  15.2 4.5 %collective-permute-done.3.rest = bf16[2,3,2,8,1024]{4,3,2,1,0:T(8,128)(2,1)S(1)} collective-permute-done((bf16[2,3,2,8,1024]{4,3,2,1,0:T(8,128)(2,1)S(1)}, bf16[2,3,2,8,1024]{4,3,2,1,0:T(8,128)(2,1)S(1)}, u32[]{:S(2)}, u32[]{:S(2)}) %collective-permute-start.3) | collective-permute-done | bytes 196640 | tf_op jit(solution)/shard_map/ppermute | solution.py:46
  24.7 1.8 collective-permute-start.11
  26.9 3.6 %collective-permute-done.9.p1 = bf16[3,8,8,1024]{3,2,1,0:T(8,128)(2,1)S(1)} collective-permute-done((bf16[3,8,8,1024]{3,2,1,0:T(8,128)(2,1)S(1)}, bf16[3,8,8,1024]{3,2,1,0:T(8,128)(2,1)S(1)}, u32[]{:S(2)}, u32[]{:S(2)}) %collective-permute-start.9) | collective-permute-done | bytes 393248 | tf_op jit(solution)/shard_map/ppermute | solution.py:46
  32.9 3.8 %collective-permute-done.12.p2 = bf16[3,8,8,1024]{3,2,1,0:T(8,128)(2,1)S(1)} collective-permute-done((bf16[3,8,8,1024]{3,2,1,0:T(8,128)(2,1)S(1)}, bf16[3,8,8,1024]{3,2,1,0:T(8,128)(2,1)S(1)}, u32[]{:S(2)}, u32[]{:S(2)}) %collective-permute-start.12) | collective-permute-done | bytes 393248 | tf_op jit(solution)/shard_map/ppermute | solution.py:46
  37.4 1.9 collective-permute-done.14.p2
  39.3 2.2 %collective-permute-done.15.p3 = bf16[3,8,8,1024]{3,2,1,0:T(8,128)(2,1)S(1)} collective-permute-done((bf16[3,8,8,1024]{3,2,1,0:T(8,128)(2,1)S(1)}, bf16[3,8,8,1024]{3,2,1,0:T(8,128)(2,1)S(1)}, u32[]{:S(2)}, u32[]{:S(2)}) %collective-permute-start.15) | collective-permute-done | bytes 393248 | tf_op jit(solution)/shard_map/ppermute | solution.py:46
  42.0 1.9 collective-permute-done.17.p3
  45.8 2.4 %collective-permute-start.18 = (bf16[2,3,4,8,1024]{4,3,2,1,0:T(8,128)(2,1)S(1)}, bf16[2,3,4,8,1024]{4,3,2,1,0:T(8,128)(2,1)S(1)}, u32[]{:S(2)}, u32[]{:S(2)}) collective-permute-start(bf16[2,3,4,8,1024]{4,3,2,1,0:T(8,128)(2,1)S(1)} %get-tuple-element.175), channel_id=1, source_target_pairs={{0,32},{1,97},{2,34},{3,99},{4,36},{5,101},{6,38},{7,103},{8,40},{... | collective-permute-start | bytes 1179656 | tf_op jit(solution)/shard_map/ppermute | solution.py:46
  48.2 1.5 collective-permute-start.20
  51.6 2.2 %collective-permute-done.18 = bf16[2,3,4,8,1024]{4,3,2,1,0:T(8,128)(2,1)S(1)} collective-permute-done((bf16[2,3,4,8,1024]{4,3,2,1,0:T(8,128)(2,1)S(1)}, bf16[2,3,4,8,1024]{4,3,2,1,0:T(8,128)(2,1)S(1)}, u32[]{:S(2)}, u32[]{:S(2)}) %collective-permute-start.18) | collective-permute-done | bytes 393248 | tf_op jit(solution)/shard_map/ppermute | solution.py:46
  53.7 2.1 %collective-permute-start.23 = (bf16[2,3,4,8,1024]{4,3,2,1,0:T(8,128)(2,1)S(1)}, bf16[2,3,4,8,1024]{4,3,2,1,0:T(8,128)(2,1)S(1)}, u32[]{:S(2)}, u32[]{:S(2)}) collective-permute-start(bf16[2,3,4,8,1024]{4,3,2,1,0:T(8,128)(2,1)S(1)} %get-tuple-element.181), channel_id=1, source_target_pairs={{0,4},{1,5},{2,6},{3,7},{4,0},{5,1},{6,2},{7,3},{8,12},{9,13},{10,... | collective-permute-start | bytes 1179656 | tf_op jit(solution)/shard_map/ppermute | solution.py:46
  57.3 1.9 collective-permute-done.20
  59.1 1.7 collective-permute-start.25
  60.9 3.0 %collective-permute-start.26 = (bf16[2,3,4,8,1024]{4,3,2,1,0:T(8,128)(2,1)S(1)}, bf16[2,3,4,8,1024]{4,3,2,1,0:T(8,128)(2,1)S(1)}, u32[]{:S(2)}, u32[]{:S(2)}) collective-permute-start(bf16[2,3,4,8,1024]{4,3,2,1,0:T(8,128)(2,1)S(1)} %get-tuple-element.185), channel_id=1, source_target_pairs={{0,16},{1,17},{2,18},{3,19},{4,20},{5,21},{6,22},{7,23},{8,24},{9,... | collective-permute-start | bytes 1179656 | tf_op jit(solution)/shard_map/ppermute | solution.py:46
  64.0 2.3 %collective-permute-done.25 = bf16[2,3,4,8,1024]{4,3,2,1,0:T(8,128)(2,1)S(1)} collective-permute-done((bf16[2,3,4,8,1024]{4,3,2,1,0:T(8,128)(2,1)S(1)}, bf16[2,3,4,8,1024]{4,3,2,1,0:T(8,128)(2,1)S(1)}, u32[]{:S(2)}, u32[]{:S(2)}) %collective-permute-start.25) | collective-permute-done | bytes 393248 | tf_op jit(solution)/shard_map/ppermute | solution.py:46
  66.3 6.9 %collective-permute-done.26 = bf16[2,3,4,8,1024]{4,3,2,1,0:T(8,128)(2,1)S(1)} collective-permute-done((bf16[2,3,4,8,1024]{4,3,2,1,0:T(8,128)(2,1)S(1)}, bf16[2,3,4,8,1024]{4,3,2,1,0:T(8,128)(2,1)S(1)}, u32[]{:S(2)}, u32[]{:S(2)}) %collective-permute-start.26) | collective-permute-done | bytes 393248 | tf_op jit(solution)/shard_map/ppermute | solution.py:46
  73.2 4.1 %first.3 = (f32[3,1024,128]{2,1,0:T(8,128)S(1)}, bf16[2,3,4,32,1024]{4,3,2,1,0:T(8,128)(2,1)S(1)}) custom-call(s32[9]{0:T(128)S(1)} %get-tuple-element.284.table_ref, bf16[512,2048]{1,0:T(8,128)(2,1)S(1)} %copy-done, bf16[512,2048]{1,0:T(8,128)(2,1)S(1)} %collective-permute-done.6.tok1, bf16[512,2048]{1,0:T(8,128)(2,1)S(1)} %copy-done.1, ...), custom_call_target="tpu_custom_call" | custom-call | tf_op jit(solution)/shard_map/first/pallas_call | solution.py:194
  77.3 10.2 %collective-permute-start.27 = (f32[3,1024,128]{2,1,0:T(8,128)S(1)}, f32[3,1024,128]{2,1,0:T(8,128)S(1)}, u32[]{:S(2)}, u32[]{:S(2)}) collective-permute-start(f32[3,1024,128]{2,1,0:T(8,128)S(1)} %get-tuple-element.190.sums), channel_id=1, source_target_pairs={{0,1},{1,0},{2,3},{3,2},{4,5},{5,4},{6,7},{7,6},{8,9},{9,8},{10,11... | collective-permute-start | bytes 4718600 | tf_op jit(solution)/shard_map/ppermute | solution.py:50
  87.4 4.1 %first.4 = (f32[3,1024,128]{2,1,0:T(8,128)S(1)}, bf16[2,3,4,32,1024]{4,3,2,1,0:T(8,128)(2,1)S(1)}) custom-call(s32[9]{0:T(128)S(1)} %get-tuple-element.283.table_ref, bf16[512,2048]{1,0:T(8,128)(2,1)S(1)} %copy-done, bf16[512,2048]{1,0:T(8,128)(2,1)S(1)} %collective-permute-done.6.tok1, bf16[512,2048]{1,0:T(8,128)(2,1)S(1)} %copy-done.1, ...), custom_call_target="tpu_custom_call" | custom-call | tf_op jit(solution)/shard_map/first/pallas_call | solution.py:194
  91.6 4.1 %first.5 = (f32[3,1024,128]{2,1,0:T(8,128)S(1)}, bf16[2,3,4,32,1024]{4,3,2,1,0:T(8,128)(2,1)S(1)}) custom-call(s32[9]{0:T(128)S(1)} %get-tuple-element.282.table_ref, bf16[512,2048]{1,0:T(8,128)(2,1)S(1)} %copy-done, bf16[512,2048]{1,0:T(8,128)(2,1)S(1)} %collective-permute-done.6.tok1, bf16[512,2048]{1,0:T(8,128)(2,1)S(1)} %copy-done.1, ...), custom_call_target="tpu_custom_call" | custom-call | tf_op jit(solution)/shard_map/first/pallas_call | solution.py:194
  96.3 3.9 %second.3 = (bf16[2,3,32,1024]{3,2,1,0:T(8,128)(2,1)S(1)}, bf16[2,3,32,1024]{3,2,1,0:T(8,128)(2,1)S(1)}, bf16[2,3,32,1024]{3,2,1,0:T(8,128)(2,1)S(1)}, bf16[2,3,...) custom-call(s32[9]{0:T(128)S(1)} %get-tuple-element.284.table_ref, ...), custom_call_target="tpu_custom_call" | custom-call | tf_op jit(solution)/shard_map/second/pallas_call | solution.py:255
  100.1 2.8 %collective-permute-start.28 = (bf16[2,3,32,1024]{3,2,1,0:T(8,128)(2,1)S(1)}, bf16[2,3,32,1024]{3,2,1,0:T(8,128)(2,1)S(1)}, u32[]{:S(2)}, u32[]{:S(2)}) collective-permute-start(bf16[2,3,32,1024]{3,2,1,0:T(8,128)(2,1)S(1)} %get-tuple-element.192), channel_id=1, source_target_pairs={{0,32},{1,97},{2,34},{3,99},{4,36},{5,101},{6,38},{7,103},{8,40},{... | collective-permute-start | bytes 1179656 | tf_op jit(solution)/shard_map/ppermute | solution.py:46
  104.2 3.9 %second.4 = (bf16[2,3,32,1024]{3,2,1,0:T(8,128)(2,1)S(1)}, bf16[2,3,32,1024]{3,2,1,0:T(8,128)(2,1)S(1)}, bf16[2,3,32,1024]{3,2,1,0:T(8,128)(2,1)S(1)}, bf16[2,3,...) custom-call(s32[9]{0:T(128)S(1)} %get-tuple-element.283.table_ref, ...), custom_call_target="tpu_custom_call" | custom-call | tf_op jit(solution)/shard_map/second/pallas_call | solution.py:255
  108.7 2.1 %collective-permute-start.34 = (bf16[2,3,32,1024]{3,2,1,0:T(8,128)(2,1)S(1)}, bf16[2,3,32,1024]{3,2,1,0:T(8,128)(2,1)S(1)}, u32[]{:S(2)}, u32[]{:S(2)}) collective-permute-start(bf16[2,3,32,1024]{3,2,1,0:T(8,128)(2,1)S(1)} %get-tuple-element.204), channel_id=1, source_target_pairs={{0,6},{1,3},{2,4},{3,1},{4,2},{5,7},{6,0},{7,5},{8,14},{9,11},{10,... | collective-permute-start | bytes 1179656 | tf_op jit(solution)/shard_map/ppermute | solution.py:46
  110.8 2.5 %collective-permute-done.28 = bf16[2,3,32,1024]{3,2,1,0:T(8,128)(2,1)S(1)} collective-permute-done((bf16[2,3,32,1024]{3,2,1,0:T(8,128)(2,1)S(1)}, bf16[2,3,32,1024]{3,2,1,0:T(8,128)(2,1)S(1)}, u32[]{:S(2)}, u32[]{:S(2)}) %collective-permute-start.28) | collective-permute-done | bytes 393248 | tf_op jit(solution)/shard_map/ppermute | solution.py:46
  113.4 9.4 %collective-permute-start.35 = (bf16[2,3,32,1024]{3,2,1,0:T(8,128)(2,1)S(1)}, bf16[2,3,32,1024]{3,2,1,0:T(8,128)(2,1)S(1)}, u32[]{:S(2)}, u32[]{:S(2)}) collective-permute-start(bf16[2,3,32,1024]{3,2,1,0:T(8,128)(2,1)S(1)} %get-tuple-element.205), channel_id=1, source_target_pairs={{0,4},{1,5},{2,6},{3,7},{4,0},{5,1},{6,2},{7,3},{8,12},{9,13},{10,... | collective-permute-start | bytes 1179656 | tf_op jit(solution)/shard_map/ppermute | solution.py:46
  122.7 3.9 %second.5 = (bf16[2,3,32,1024]{3,2,1,0:T(8,128)(2,1)S(1)}, bf16[2,3,32,1024]{3,2,1,0:T(8,128)(2,1)S(1)}, bf16[2,3,32,1024]{3,2,1,0:T(8,128)(2,1)S(1)}, bf16[2,3,...) custom-call(s32[9]{0:T(128)S(1)} %get-tuple-element.282.table_ref, ...), custom_call_target="tpu_custom_call" | custom-call | tf_op jit(solution)/shard_map/second/pallas_call | solution.py:255
  126.6 10.1 %collective-permute-start.38 = (bf16[2,3,32,1024]{3,2,1,0:T(8,128)(2,1)S(1)}, bf16[2,3,32,1024]{3,2,1,0:T(8,128)(2,1)S(1)}, u32[]{:S(2)}, u32[]{:S(2)}) collective-permute-start(bf16[2,3,32,1024]{3,2,1,0:T(8,128)(2,1)S(1)} %get-tuple-element.213), channel_id=1, source_target_pairs={{0,8},{1,25},{2,10},{3,27},{4,12},{5,29},{6,14},{7,31},{8,0},{9,17... | collective-permute-start | bytes 1179656 | tf_op jit(solution)/shard_map/ppermute | solution.py:46
  136.9 3.7 %collective-permute-start.40 = (bf16[2,3,32,1024]{3,2,1,0:T(8,128)(2,1)S(1)}, bf16[2,3,32,1024]{3,2,1,0:T(8,128)(2,1)S(1)}, u32[]{:S(2)}, u32[]{:S(2)}) collective-permute-start(bf16[2,3,32,1024]{3,2,1,0:T(8,128)(2,1)S(1)} %get-tuple-element.215), channel_id=1, source_target_pairs={{0,16},{1,17},{2,18},{3,19},{4,20},{5,21},{6,22},{7,23},{8,24},{9,... | collective-permute-start | bytes 1179656 | tf_op jit(solution)/shard_map/ppermute | solution.py:46
  143.2 11.4 %collective-permute-done.38 = bf16[2,3,32,1024]{3,2,1,0:T(8,128)(2,1)S(1)} collective-permute-done((bf16[2,3,32,1024]{3,2,1,0:T(8,128)(2,1)S(1)}, bf16[2,3,32,1024]{3,2,1,0:T(8,128)(2,1)S(1)}, u32[]{:S(2)}, u32[]{:S(2)}) %collective-permute-start.38) | collective-permute-done | bytes 393248 | tf_op jit(solution)/shard_map/ppermute | solution.py:46
  155.8 2.1 %collective-permute-start.41 = (bf16[2,3,8,8,1024]{4,3,2,1,0:T(8,128)(2,1)S(1)}, bf16[2,3,8,8,1024]{4,3,2,1,0:T(8,128)(2,1)S(1)}, u32[]{:S(2)}, u32[]{:S(2)}) collective-permute-start(bf16[2,3,8,8,1024]{4,3,2,1,0:T(8,128)(2,1)S(1)} %get-tuple-element.216), channel_id=1, source_target_pairs={{0,6},{1,3},{2,4},{3,1},{4,2},{5,7},{6,0},{7,5},{8,14},{9,11},{10,... | collective-permute-start | bytes 2359304 | tf_op jit(solution)/shard_map/ppermute | solution.py:46
  157.9 3.1 %rows_out.2 = (bf16[512,1024]{1,0:T(8,128)(2,1)S(1)}, bf16[512,1024]{1,0:T(8,128)(2,1)S(1)}) custom-call(s32[9]{0:T(128)S(1)} %get-tuple-element.284.table_ref, bf16[1024,256]{1,0:T(8,128)(2,1)S(1)} %get-tuple-element.240.refs_0_, bf16[1024,256]{1,0:T(8,128)(2,1)S(1)} %get-tuple-element.241.refs_1_, bf16[1024,256]{1,0:T(8,128)(2,1)S(1)} %get-tuple-element.242.refs_2_, ...), custom_call_target="tpu_custom_call" | custom-call | tf_op jit(solution)/shard_map/rows_out/pallas_call | solution.py:297
  161.6 5.9 %collective-permute-done.41.came = bf16[2,3,8,8,1024]{4,3,2,1,0:T(8,128)(2,1)S(1)} collective-permute-done((bf16[2,3,8,8,1024]{4,3,2,1,0:T(8,128)(2,1)S(1)}, bf16[2,3,8,8,1024]{4,3,2,1,0:T(8,128)(2,1)S(1)}, u32[]{:S(2)}, u32[]{:S(2)}) %collective-permute-start.41) | collective-permute-done | bytes 786464 | tf_op jit(solution)/shard_map/ppermute | solution.py:46
  168.0 2.4 %collective-permute-start.42 = (bf16[3,8,8,1024]{3,2,1,0:T(8,128)(2,1)S(1)}, bf16[3,8,8,1024]{3,2,1,0:T(8,128)(2,1)S(1)}, u32[]{:S(2)}, u32[]{:S(2)}) collective-permute-start(bf16[3,8,8,1024]{3,2,1,0:T(8,128)(2,1)S(1)} %fusion.2), channel_id=1, source_target_pairs={{0,8},{1,25},{2,10},{3,27},{4,12},{5,29},{6,14},{7,31},{8,0},{9,17... | collective-permute-start | bytes 1179656 | tf_op jit(solution)/shard_map/ppermute | solution.py:46
  170.3 3.3 %collective-permute-start.43 = (bf16[3,8,8,1024]{3,2,1,0:T(8,128)(2,1)S(1)}, bf16[3,8,8,1024]{3,2,1,0:T(8,128)(2,1)S(1)}, u32[]{:S(2)}, u32[]{:S(2)}) collective-permute-start(bf16[3,8,8,1024]{3,2,1,0:T(8,128)(2,1)S(1)} %get-tuple-element.224), channel_id=1, source_target_pairs={{0,32},{1,97},{2,34},{3,99},{4,36},{5,101},{6,38},{7,103},{8,40},{... | collective-permute-start | bytes 1179656 | tf_op jit(solution)/shard_map/ppermute | solution.py:46
  174.1 5.0 %rows_out.3 = (bf16[512,2048]{1,0:T(8,128)(2,1)}, bf16[512,2048]{1,0:T(8,128)(2,1)}) custom-call(s32[9]{0:T(128)S(1)} %get-tuple-element.284.table_ref, bf16[1024,256]{1,0:T(8,128)(2,1)S(1)} %get-tuple-element.240.refs_0_, bf16[1024,256]{1,0:T(8,128)(2,1)S(1)} %get-tuple-element.241.refs_1_, bf16[1024,256]{1,0:T(8,128)(2,1)S(1)} %get-tuple-element.242.refs_2_, ...), custom_call_target="tpu_custom_call" | custom-call | tf_op jit(solution)/shard_map/rows_out/pallas_call | solution.py:297
  179.1 2.3 %collective-permute-done.44.last = bf16[3,8,8,1024]{3,2,1,0:T(8,128)(2,1)S(1)} collective-permute-done((bf16[3,8,8,1024]{3,2,1,0:T(8,128)(2,1)S(1)}, bf16[3,8,8,1024]{3,2,1,0:T(8,128)(2,1)S(1)}, u32[]{:S(2)}, u32[]{:S(2)}) %collective-permute-start.44) | collective-permute-done | bytes 393248 | tf_op jit(solution)/shard_map/ppermute | solution.py:46
  181.5 1.7 unweave.5
  183.1 1.7 unweave.4
  184.8 1.7 unweave.3
  186.8 4.3 %collective-permute-done.47 = bf16[2,3,2,8,1024]{4,3,2,1,0:T(8,128)(2,1)S(1)} collective-permute-done((bf16[2,3,2,8,1024]{4,3,2,1,0:T(8,128)(2,1)S(1)}, bf16[2,3,2,8,1024]{4,3,2,1,0:T(8,128)(2,1)S(1)}, u32[]{:S(2)}, u32[]{:S(2)}) %collective-permute-start.47) | collective-permute-done | bytes 196640 | tf_op jit(solution)/shard_map/ppermute | solution.py:46
  193.9 2.3 %collective-permute-done.50 = bf16[3,2,8,1024]{3,2,1,0:T(8,128)(2,1)S(1)} collective-permute-done((bf16[3,2,8,1024]{3,2,1,0:T(8,128)(2,1)S(1)}, bf16[3,2,8,1024]{3,2,1,0:T(8,128)(2,1)S(1)}, u32[]{:S(2)}, u32[]{:S(2)}) %collective-permute-start.50) | collective-permute-done | bytes 98336 | tf_op jit(solution)/shard_map/ppermute | solution.py:46
  197.7 1.5 divide_subtract_fusion
  (117 shorter events, 28.7 us)
Async XLA Ops:
  0.7 19.3 %collective-permute-start.6 = (bf16[512,2048]{1,0:T(8,128)(2,1)}, bf16[512,2048]{1,0:T(8,128)(2,1)S(1)}, u32[]{:S(2)}, u32[]{:S(2)}) collective-permute-start(bf16[512,2048]{1,0:T(8,128)(2,1)} %tok0.5), channel_id=1, source_target_pairs={{0,1},{1,0},{2,3},{3,2},{4,5},{5,4},{6,7},{7,6},{8,9},{9,8},{10,11... | collective-permute-start | bytes 6291464 | tf_op jit(solution)/shard_map/ppermute | solution.py:50
  2.2 17.8 %collective-permute-start.7 = (bf16[512,2048]{1,0:T(8,128)(2,1)}, bf16[512,2048]{1,0:T(8,128)(2,1)}, u32[]{:S(2)}, u32[]{:S(2)}) collective-permute-start(bf16[512,2048]{1,0:T(8,128)(2,1)} %cot0.5), channel_id=1, source_target_pairs={{0,1},{1,0},{2,3},{3,2},{4,5},{5,4},{6,7},{7,6},{8,9},{9,8},{10,11... | collective-permute-start | bytes 6291464 | tf_op jit(solution)/shard_map/ppermute | solution.py:50
  3.4 9.6 %collective-permute-start.2 = (bf16[3,2,8,1024]{3,2,1,0:T(8,128)(2,1)S(1)}, bf16[3,2,8,1024]{3,2,1,0:T(8,128)(2,1)S(1)}, u32[]{:S(2)}, u32[]{:S(2)}) collective-permute-start(bf16[3,2,8,1024]{3,2,1,0:T(8,128)(2,1)S(1)} %get-tuple-element.279.own), channel_id=1, source_target_pairs={{0,32},{1,97},{2,34},{3,99},{4,36},{5,101},{6,38},{7,103},{8,40},{... | collective-permute-start | bytes 294920 | tf_op jit(solution)/shard_map/ppermute | solution.py:46
  7.4 5.8 %collective-permute-start.1 = (bf16[3,2,8,1024]{3,2,1,0:T(8,128)(2,1)S(1)}, bf16[3,2,8,1024]{3,2,1,0:T(8,128)(2,1)S(1)}, u32[]{:S(2)}, u32[]{:S(2)}) collective-permute-start(bf16[3,2,8,1024]{3,2,1,0:T(8,128)(2,1)S(1)} %get-tuple-element.280.own), channel_id=1, source_target_pairs={{0,8},{1,25},{2,10},{3,27},{4,12},{5,29},{6,14},{7,31},{8,0},{9,17... | collective-permute-start | bytes 294920 | tf_op jit(solution)/shard_map/ppermute | solution.py:46
  10.1 4.7 %collective-permute-start = (bf16[3,2,8,1024]{3,2,1,0:T(8,128)(2,1)S(1)}, bf16[3,2,8,1024]{3,2,1,0:T(8,128)(2,1)S(1)}, u32[]{:S(2)}, u32[]{:S(2)}) collective-permute-start(bf16[3,2,8,1024]{3,2,1,0:T(8,128)(2,1)S(1)} %get-tuple-element.281.own), channel_id=1, source_target_pairs={{0,2},{1,7},{2,0},{3,5},{4,6},{5,3},{6,4},{7,1},{8,10},{9,15},{10,... | collective-permute-start | bytes 294920 | tf_op jit(solution)/shard_map/ppermute | solution.py:46
  14.8 4.9 %collective-permute-start.3 = (bf16[2,3,2,8,1024]{4,3,2,1,0:T(8,128)(2,1)S(1)}, bf16[2,3,2,8,1024]{4,3,2,1,0:T(8,128)(2,1)S(1)}, u32[]{:S(2)}, u32[]{:S(2)}) collective-permute-start(bf16[2,3,2,8,1024]{4,3,2,1,0:T(8,128)(2,1)S(1)} %pad_maximum_fusion.1), channel_id=1, source_target_pairs={{0,6},{1,3},{2,4},{3,1},{4,2},{5,7},{6,0},{7,5},{8,14},{9,11},{10,... | collective-permute-start | bytes 589832 | tf_op jit(solution)/shard_map/ppermute | solution.py:46
  14.9 4.9 %collective-permute-start.4 = (bf16[2,3,2,8,1024]{4,3,2,1,0:T(8,128)(2,1)S(1)}, bf16[2,3,2,8,1024]{4,3,2,1,0:T(8,128)(2,1)S(1)}, u32[]{:S(2)}, u32[]{:S(2)}) collective-permute-start(bf16[2,3,2,8,1024]{4,3,2,1,0:T(8,128)(2,1)S(1)} %pad_maximum_fusion.2), channel_id=1, source_target_pairs={{0,24},{1,9},{2,26},{3,11},{4,28},{5,13},{6,30},{7,15},{8,16},{9,1... | collective-permute-start | bytes 589832 | tf_op jit(solution)/shard_map/ppermute | solution.py:46
  15.1 4.9 %collective-permute-start.5 = (bf16[2,3,2,8,1024]{4,3,2,1,0:T(8,128)(2,1)S(1)}, bf16[2,3,2,8,1024]{4,3,2,1,0:T(8,128)(2,1)S(1)}, u32[]{:S(2)}, u32[]{:S(2)}) collective-permute-start(bf16[2,3,2,8,1024]{4,3,2,1,0:T(8,128)(2,1)S(1)} %pad_maximum_fusion.3), channel_id=1, source_target_pairs={{0,96},{1,33},{2,98},{3,35},{4,100},{5,37},{6,102},{7,39},{8,104},... | collective-permute-start | bytes 589832 | tf_op jit(solution)/shard_map/ppermute | solution.py:46
  22.6 7.9 %collective-permute-start.9 = (bf16[3,8,8,1024]{3,2,1,0:T(8,128)(2,1)S(1)}, bf16[3,8,8,1024]{3,2,1,0:T(8,128)(2,1)S(1)}, u32[]{:S(2)}, u32[]{:S(2)}) collective-permute-start(bf16[3,8,8,1024]{3,2,1,0:T(8,128)(2,1)S(1)} %weave.3.p0), channel_id=1, source_target_pairs={{0,8},{1,25},{2,10},{3,27},{4,12},{5,29},{6,14},{7,31},{8,0},{9,17... | collective-permute-start | bytes 1179656 | tf_op jit(solution)/shard_map/ppermute | solution.py:46
  23.6 8.4 %collective-permute-start.10 = (bf16[3,8,8,1024]{3,2,1,0:T(8,128)(2,1)S(1)}, bf16[3,8,8,1024]{3,2,1,0:T(8,128)(2,1)S(1)}, u32[]{:S(2)}, u32[]{:S(2)}) collective-permute-start(bf16[3,8,8,1024]{3,2,1,0:T(8,128)(2,1)S(1)} %weave.4.p0), channel_id=1, source_target_pairs={{0,32},{1,97},{2,34},{3,99},{4,36},{5,101},{6,38},{7,103},{8,40},{... | collective-permute-start | bytes 1179656 | tf_op jit(solution)/shard_map/ppermute | solution.py:46
  24.7 8.1 %collective-permute-start.11 = (bf16[3,8,8,1024]{3,2,1,0:T(8,128)(2,1)S(1)}, bf16[3,8,8,1024]{3,2,1,0:T(8,128)(2,1)S(1)}, u32[]{:S(2)}, u32[]{:S(2)}) collective-permute-start(bf16[3,8,8,1024]{3,2,1,0:T(8,128)(2,1)S(1)} %weave.5.p0), channel_id=1, source_target_pairs={{0,2},{1,7},{2,0},{3,5},{4,6},{5,3},{6,4},{7,1},{8,10},{9,15},{10,... | collective-permute-start | bytes 1179656 | tf_op jit(solution)/shard_map/ppermute | solution.py:46
  26.5 10.2 %collective-permute-start.12 = (bf16[3,8,8,1024]{3,2,1,0:T(8,128)(2,1)S(1)}, bf16[3,8,8,1024]{3,2,1,0:T(8,128)(2,1)S(1)}, u32[]{:S(2)}, u32[]{:S(2)}) collective-permute-start(bf16[3,8,8,1024]{3,2,1,0:T(8,128)(2,1)S(1)} %weave.3.p0), channel_id=1, source_target_pairs={{0,24},{1,9},{2,26},{3,11},{4,28},{5,13},{6,30},{7,15},{8,16},{9,1... | collective-permute-start | bytes 1179656 | tf_op jit(solution)/shard_map/ppermute | solution.py:46
  26.9 10.5 %collective-permute-start.13 = (bf16[3,8,8,1024]{3,2,1,0:T(8,128)(2,1)S(1)}, bf16[3,8,8,1024]{3,2,1,0:T(8,128)(2,1)S(1)}, u32[]{:S(2)}, u32[]{:S(2)}) collective-permute-start(bf16[3,8,8,1024]{3,2,1,0:T(8,128)(2,1)S(1)} %weave.4.p0), channel_id=1, source_target_pairs={{0,96},{1,33},{2,98},{3,35},{4,100},{5,37},{6,102},{7,39},{8,104},... | collective-permute-start | bytes 1179656 | tf_op jit(solution)/shard_map/ppermute | solution.py:46
  30.5 8.8 %collective-permute-start.14 = (bf16[3,8,8,1024]{3,2,1,0:T(8,128)(2,1)S(1)}, bf16[3,8,8,1024]{3,2,1,0:T(8,128)(2,1)S(1)}, u32[]{:S(2)}, u32[]{:S(2)}) collective-permute-start(bf16[3,8,8,1024]{3,2,1,0:T(8,128)(2,1)S(1)} %weave.5.p0), channel_id=1, source_target_pairs={{0,6},{1,3},{2,4},{3,1},{4,2},{5,7},{6,0},{7,5},{8,14},{9,11},{10,... | collective-permute-start | bytes 1179656 | tf_op jit(solution)/shard_map/ppermute | solution.py:46
  32.8 8.7 %collective-permute-start.15 = (bf16[3,8,8,1024]{3,2,1,0:T(8,128)(2,1)S(1)}, bf16[3,8,8,1024]{3,2,1,0:T(8,128)(2,1)S(1)}, u32[]{:S(2)}, u32[]{:S(2)}) collective-permute-start(bf16[3,8,8,1024]{3,2,1,0:T(8,128)(2,1)S(1)} %collective-permute-done.9.p1), channel_id=1, source_target_pairs={{0,24},{1,9},{2,26},{3,11},{4,28},{5,13},{6,30},{7,15},{8,16},{9,1... | collective-permute-start | bytes 1179656 | tf_op jit(solution)/shard_map/ppermute | solution.py:46
  32.9 9.0 %collective-permute-start.16 = (bf16[3,8,8,1024]{3,2,1,0:T(8,128)(2,1)S(1)}, bf16[3,8,8,1024]{3,2,1,0:T(8,128)(2,1)S(1)}, u32[]{:S(2)}, u32[]{:S(2)}) collective-permute-start(bf16[3,8,8,1024]{3,2,1,0:T(8,128)(2,1)S(1)} %collective-permute-done.10.p1), channel_id=1, source_target_pairs={{0,96},{1,33},{2,98},{3,35},{4,100},{5,37},{6,102},{7,39},{8,104},... | collective-permute-start | bytes 1179656 | tf_op jit(solution)/shard_map/ppermute | solution.py:46
  36.7 7.1 %collective-permute-start.17 = (bf16[3,8,8,1024]{3,2,1,0:T(8,128)(2,1)S(1)}, bf16[3,8,8,1024]{3,2,1,0:T(8,128)(2,1)S(1)}, u32[]{:S(2)}, u32[]{:S(2)}) collective-permute-start(bf16[3,8,8,1024]{3,2,1,0:T(8,128)(2,1)S(1)} %collective-permute-done.11.p1), channel_id=1, source_target_pairs={{0,6},{1,3},{2,4},{3,1},{4,2},{5,7},{6,0},{7,5},{8,14},{9,11},{10,... | collective-permute-start | bytes 1179656 | tf_op jit(solution)/shard_map/ppermute | solution.py:46
  45.8 7.9 %collective-permute-start.18 = (bf16[2,3,4,8,1024]{4,3,2,1,0:T(8,128)(2,1)S(1)}, bf16[2,3,4,8,1024]{4,3,2,1,0:T(8,128)(2,1)S(1)}, u32[]{:S(2)}, u32[]{:S(2)}) collective-permute-start(bf16[2,3,4,8,1024]{4,3,2,1,0:T(8,128)(2,1)S(1)} %get-tuple-element.175), channel_id=1, source_target_pairs={{0,32},{1,97},{2,34},{3,99},{4,36},{5,101},{6,38},{7,103},{8,40},{... | collective-permute-start | bytes 1179656 | tf_op jit(solution)/shard_map/ppermute | solution.py:46
  48.2 7.6 %collective-permute-start.19 = (bf16[2,3,4,8,1024]{4,3,2,1,0:T(8,128)(2,1)S(1)}, bf16[2,3,4,8,1024]{4,3,2,1,0:T(8,128)(2,1)S(1)}, u32[]{:S(2)}, u32[]{:S(2)}) collective-permute-start(bf16[2,3,4,8,1024]{4,3,2,1,0:T(8,128)(2,1)S(1)} %get-tuple-element.176), channel_id=1, source_target_pairs={{0,96},{1,33},{2,98},{3,35},{4,100},{5,37},{6,102},{7,39},{8,104},... | collective-permute-start | bytes 1179656 | tf_op jit(solution)/shard_map/ppermute | solution.py:46
  48.2 10.9 %collective-permute-start.20 = (bf16[2,3,4,8,1024]{4,3,2,1,0:T(8,128)(2,1)S(1)}, bf16[2,3,4,8,1024]{4,3,2,1,0:T(8,128)(2,1)S(1)}, u32[]{:S(2)}, u32[]{:S(2)}) collective-permute-start(bf16[2,3,4,8,1024]{4,3,2,1,0:T(8,128)(2,1)S(1)} %get-tuple-element.177), channel_id=1, source_target_pairs={{0,64},{1,65},{2,66},{3,67},{4,68},{5,69},{6,70},{7,71},{8,72},{9,... | collective-permute-start | bytes 1179656 | tf_op jit(solution)/shard_map/ppermute | solution.py:46
  49.8 11.1 %collective-permute-start.21 = (bf16[2,3,4,8,1024]{4,3,2,1,0:T(8,128)(2,1)S(1)}, bf16[2,3,4,8,1024]{4,3,2,1,0:T(8,128)(2,1)S(1)}, u32[]{:S(2)}, u32[]{:S(2)}) collective-permute-start(bf16[2,3,4,8,1024]{4,3,2,1,0:T(8,128)(2,1)S(1)} %get-tuple-element.179), channel_id=1, source_target_pairs={{0,2},{1,7},{2,0},{3,5},{4,6},{5,3},{6,4},{7,1},{8,10},{9,15},{10,... | collective-permute-start | bytes 1179656 | tf_op jit(solution)/shard_map/ppermute | solution.py:46
  51.1 12.8 %collective-permute-start.22 = (bf16[2,3,4,8,1024]{4,3,2,1,0:T(8,128)(2,1)S(1)}, bf16[2,3,4,8,1024]{4,3,2,1,0:T(8,128)(2,1)S(1)}, u32[]{:S(2)}, u32[]{:S(2)}) collective-permute-start(bf16[2,3,4,8,1024]{4,3,2,1,0:T(8,128)(2,1)S(1)} %get-tuple-element.180), channel_id=1, source_target_pairs={{0,6},{1,3},{2,4},{3,1},{4,2},{5,7},{6,0},{7,5},{8,14},{9,11},{10,... | collective-permute-start | bytes 1179656 | tf_op jit(solution)/shard_map/ppermute | solution.py:46
  53.7 10.1 %collective-permute-start.23 = (bf16[2,3,4,8,1024]{4,3,2,1,0:T(8,128)(2,1)S(1)}, bf16[2,3,4,8,1024]{4,3,2,1,0:T(8,128)(2,1)S(1)}, u32[]{:S(2)}, u32[]{:S(2)}) collective-permute-start(bf16[2,3,4,8,1024]{4,3,2,1,0:T(8,128)(2,1)S(1)} %get-tuple-element.181), channel_id=1, source_target_pairs={{0,4},{1,5},{2,6},{3,7},{4,0},{5,1},{6,2},{7,3},{8,12},{9,13},{10,... | collective-permute-start | bytes 1179656 | tf_op jit(solution)/shard_map/ppermute | solution.py:46
  55.9 8.1 %collective-permute-start.24 = (bf16[2,3,4,8,1024]{4,3,2,1,0:T(8,128)(2,1)S(1)}, bf16[2,3,4,8,1024]{4,3,2,1,0:T(8,128)(2,1)S(1)}, u32[]{:S(2)}, u32[]{:S(2)}) collective-permute-start(bf16[2,3,4,8,1024]{4,3,2,1,0:T(8,128)(2,1)S(1)} %get-tuple-element.183), channel_id=1, source_target_pairs={{0,8},{1,25},{2,10},{3,27},{4,12},{5,29},{6,14},{7,31},{8,0},{9,17... | collective-permute-start | bytes 1179656 | tf_op jit(solution)/shard_map/ppermute | solution.py:46
  59.1 7.2 %collective-permute-start.25 = (bf16[2,3,4,8,1024]{4,3,2,1,0:T(8,128)(2,1)S(1)}, bf16[2,3,4,8,1024]{4,3,2,1,0:T(8,128)(2,1)S(1)}, u32[]{:S(2)}, u32[]{:S(2)}) collective-permute-start(bf16[2,3,4,8,1024]{4,3,2,1,0:T(8,128)(2,1)S(1)} %get-tuple-element.184), channel_id=1, source_target_pairs={{0,24},{1,9},{2,26},{3,11},{4,28},{5,13},{6,30},{7,15},{8,16},{9,1... | collective-permute-start | bytes 1179656 | tf_op jit(solution)/shard_map/ppermute | solution.py:46
  60.9 12.3 %collective-permute-start.26 = (bf16[2,3,4,8,1024]{4,3,2,1,0:T(8,128)(2,1)S(1)}, bf16[2,3,4,8,1024]{4,3,2,1,0:T(8,128)(2,1)S(1)}, u32[]{:S(2)}, u32[]{:S(2)}) collective-permute-start(bf16[2,3,4,8,1024]{4,3,2,1,0:T(8,128)(2,1)S(1)} %get-tuple-element.185), channel_id=1, source_target_pairs={{0,16},{1,17},{2,18},{3,19},{4,20},{5,21},{6,22},{7,23},{8,24},{9,... | collective-permute-start | bytes 1179656 | tf_op jit(solution)/shard_map/ppermute | solution.py:46
  77.3 19.0 %collective-permute-start.27 = (f32[3,1024,128]{2,1,0:T(8,128)S(1)}, f32[3,1024,128]{2,1,0:T(8,128)S(1)}, u32[]{:S(2)}, u32[]{:S(2)}) collective-permute-start(f32[3,1024,128]{2,1,0:T(8,128)S(1)} %get-tuple-element.190.sums), channel_id=1, source_target_pairs={{0,1},{1,0},{2,3},{3,2},{4,5},{5,4},{6,7},{7,6},{8,9},{9,8},{10,11... | collective-permute-start | bytes 4718600 | tf_op jit(solution)/shard_map/ppermute | solution.py:50
  91.5 12.7 %collective-permute-start.32 = (f32[3,1024,128]{2,1,0:T(8,128)S(1)}, f32[3,1024,128]{2,1,0:T(8,128)S(1)}, u32[]{:S(2)}, u32[]{:S(2)}) collective-permute-start(f32[3,1024,128]{2,1,0:T(8,128)S(1)} %get-tuple-element.201.sums), channel_id=1, source_target_pairs={{0,1},{1,0},{2,3},{3,2},{4,5},{5,4},{6,7},{7,6},{8,9},{9,8},{10,11... | collective-permute-start | bytes 4718600 | tf_op jit(solution)/shard_map/ppermute | solution.py:50
  95.7 13.0 %collective-permute-start.37 = (f32[3,1024,128]{2,1,0:T(8,128)S(1)}, f32[3,1024,128]{2,1,0:T(8,128)S(1)}, u32[]{:S(2)}, u32[]{:S(2)}) collective-permute-start(f32[3,1024,128]{2,1,0:T(8,128)S(1)} %get-tuple-element.211.sums), channel_id=1, source_target_pairs={{0,1},{1,0},{2,3},{3,2},{4,5},{5,4},{6,7},{7,6},{8,9},{9,8},{10,11... | collective-permute-start | bytes 4718600 | tf_op jit(solution)/shard_map/ppermute | solution.py:50
  100.1 13.3 %collective-permute-start.28 = (bf16[2,3,32,1024]{3,2,1,0:T(8,128)(2,1)S(1)}, bf16[2,3,32,1024]{3,2,1,0:T(8,128)(2,1)S(1)}, u32[]{:S(2)}, u32[]{:S(2)}) collective-permute-start(bf16[2,3,32,1024]{3,2,1,0:T(8,128)(2,1)S(1)} %get-tuple-element.192), channel_id=1, source_target_pairs={{0,32},{1,97},{2,34},{3,99},{4,36},{5,101},{6,38},{7,103},{8,40},{... | collective-permute-start | bytes 1179656 | tf_op jit(solution)/shard_map/ppermute | solution.py:46
  102.9 23.7 %collective-permute-start.29 = (bf16[2,3,32,1024]{3,2,1,0:T(8,128)(2,1)S(1)}, bf16[2,3,32,1024]{3,2,1,0:T(8,128)(2,1)S(1)}, u32[]{:S(2)}, u32[]{:S(2)}) collective-permute-start(bf16[2,3,32,1024]{3,2,1,0:T(8,128)(2,1)S(1)} %get-tuple-element.193), channel_id=1, source_target_pairs={{0,96},{1,33},{2,98},{3,35},{4,100},{5,37},{6,102},{7,39},{8,104},... | collective-permute-start | bytes 1179656 | tf_op jit(solution)/shard_map/ppermute | solution.py:46
  102.9 33.9 %collective-permute-start.30 = (bf16[2,3,32,1024]{3,2,1,0:T(8,128)(2,1)S(1)}, bf16[2,3,32,1024]{3,2,1,0:T(8,128)(2,1)S(1)}, u32[]{:S(2)}, u32[]{:S(2)}) collective-permute-start(bf16[2,3,32,1024]{3,2,1,0:T(8,128)(2,1)S(1)} %get-tuple-element.194), channel_id=1, source_target_pairs={{0,64},{1,65},{2,66},{3,67},{4,68},{5,69},{6,70},{7,71},{8,72},{9,... | collective-permute-start | bytes 1179656 | tf_op jit(solution)/shard_map/ppermute | solution.py:46
  108.0 28.8 %collective-permute-start.33 = (bf16[2,3,32,1024]{3,2,1,0:T(8,128)(2,1)S(1)}, bf16[2,3,32,1024]{3,2,1,0:T(8,128)(2,1)S(1)}, u32[]{:S(2)}, u32[]{:S(2)}) collective-permute-start(bf16[2,3,32,1024]{3,2,1,0:T(8,128)(2,1)S(1)} %get-tuple-element.203), channel_id=1, source_target_pairs={{0,2},{1,7},{2,0},{3,5},{4,6},{5,3},{6,4},{7,1},{8,10},{9,15},{10,... | collective-permute-start | bytes 1179656 | tf_op jit(solution)/shard_map/ppermute | solution.py:46
  108.7 33.1 %collective-permute-start.34 = (bf16[2,3,32,1024]{3,2,1,0:T(8,128)(2,1)S(1)}, bf16[2,3,32,1024]{3,2,1,0:T(8,128)(2,1)S(1)}, u32[]{:S(2)}, u32[]{:S(2)}) collective-permute-start(bf16[2,3,32,1024]{3,2,1,0:T(8,128)(2,1)S(1)} %get-tuple-element.204), channel_id=1, source_target_pairs={{0,6},{1,3},{2,4},{3,1},{4,2},{5,7},{6,0},{7,5},{8,14},{9,11},{10,... | collective-permute-start | bytes 1179656 | tf_op jit(solution)/shard_map/ppermute | solution.py:46
  113.4 28.5 %collective-permute-start.35 = (bf16[2,3,32,1024]{3,2,1,0:T(8,128)(2,1)S(1)}, bf16[2,3,32,1024]{3,2,1,0:T(8,128)(2,1)S(1)}, u32[]{:S(2)}, u32[]{:S(2)}) collective-permute-start(bf16[2,3,32,1024]{3,2,1,0:T(8,128)(2,1)S(1)} %get-tuple-element.205), channel_id=1, source_target_pairs={{0,4},{1,5},{2,6},{3,7},{4,0},{5,1},{6,2},{7,3},{8,12},{9,13},{10,... | collective-permute-start | bytes 1179656 | tf_op jit(solution)/shard_map/ppermute | solution.py:46
  126.6 28.0 %collective-permute-start.38 = (bf16[2,3,32,1024]{3,2,1,0:T(8,128)(2,1)S(1)}, bf16[2,3,32,1024]{3,2,1,0:T(8,128)(2,1)S(1)}, u32[]{:S(2)}, u32[]{:S(2)}) collective-permute-start(bf16[2,3,32,1024]{3,2,1,0:T(8,128)(2,1)S(1)} %get-tuple-element.213), channel_id=1, source_target_pairs={{0,8},{1,25},{2,10},{3,27},{4,12},{5,29},{6,14},{7,31},{8,0},{9,17... | collective-permute-start | bytes 1179656 | tf_op jit(solution)/shard_map/ppermute | solution.py:46
  136.8 17.8 %collective-permute-start.39 = (bf16[2,3,32,1024]{3,2,1,0:T(8,128)(2,1)S(1)}, bf16[2,3,32,1024]{3,2,1,0:T(8,128)(2,1)S(1)}, u32[]{:S(2)}, u32[]{:S(2)}) collective-permute-start(bf16[2,3,32,1024]{3,2,1,0:T(8,128)(2,1)S(1)} %get-tuple-element.214), channel_id=1, source_target_pairs={{0,24},{1,9},{2,26},{3,11},{4,28},{5,13},{6,30},{7,15},{8,16},{9,1... | collective-permute-start | bytes 1179656 | tf_op jit(solution)/shard_map/ppermute | solution.py:46
  136.9 17.7 %collective-permute-start.40 = (bf16[2,3,32,1024]{3,2,1,0:T(8,128)(2,1)S(1)}, bf16[2,3,32,1024]{3,2,1,0:T(8,128)(2,1)S(1)}, u32[]{:S(2)}, u32[]{:S(2)}) collective-permute-start(bf16[2,3,32,1024]{3,2,1,0:T(8,128)(2,1)S(1)} %get-tuple-element.215), channel_id=1, source_target_pairs={{0,16},{1,17},{2,18},{3,19},{4,20},{5,21},{6,22},{7,23},{8,24},{9,... | collective-permute-start | bytes 1179656 | tf_op jit(solution)/shard_map/ppermute | solution.py:46
  141.8 19.8 %collective-permute-start.31 = (bf16[2,3,8,8,1024]{4,3,2,1,0:T(8,128)(2,1)S(1)}, bf16[2,3,8,8,1024]{4,3,2,1,0:T(8,128)(2,1)S(1)}, u32[]{:S(2)}, u32[]{:S(2)}) collective-permute-start(bf16[2,3,8,8,1024]{4,3,2,1,0:T(8,128)(2,1)S(1)} %get-tuple-element.196), channel_id=1, source_target_pairs={{0,24},{1,9},{2,26},{3,11},{4,28},{5,13},{6,30},{7,15},{8,16},{9,1... | collective-permute-start | bytes 2359304 | tf_op jit(solution)/shard_map/ppermute | solution.py:46
  143.1 18.5 %collective-permute-start.36 = (bf16[2,3,8,8,1024]{4,3,2,1,0:T(8,128)(2,1)S(1)}, bf16[2,3,8,8,1024]{4,3,2,1,0:T(8,128)(2,1)S(1)}, u32[]{:S(2)}, u32[]{:S(2)}) collective-permute-start(bf16[2,3,8,8,1024]{4,3,2,1,0:T(8,128)(2,1)S(1)} %get-tuple-element.206), channel_id=1, source_target_pairs={{0,96},{1,33},{2,98},{3,35},{4,100},{5,37},{6,102},{7,39},{8,104},... | collective-permute-start | bytes 2359304 | tf_op jit(solution)/shard_map/ppermute | solution.py:46
  155.8 11.7 %collective-permute-start.41 = (bf16[2,3,8,8,1024]{4,3,2,1,0:T(8,128)(2,1)S(1)}, bf16[2,3,8,8,1024]{4,3,2,1,0:T(8,128)(2,1)S(1)}, u32[]{:S(2)}, u32[]{:S(2)}) collective-permute-start(bf16[2,3,8,8,1024]{4,3,2,1,0:T(8,128)(2,1)S(1)} %get-tuple-element.216), channel_id=1, source_target_pairs={{0,6},{1,3},{2,4},{3,1},{4,2},{5,7},{6,0},{7,5},{8,14},{9,11},{10,... | collective-permute-start | bytes 2359304 | tf_op jit(solution)/shard_map/ppermute | solution.py:46
  161.0 13.1 %collective-permute-start.45 = (bf16[512,1024]{1,0:T(8,128)(2,1)S(1)}, bf16[512,1024]{1,0:T(8,128)(2,1)S(1)}, u32[]{:S(2)}, u32[]{:S(2)}) collective-permute-start(bf16[512,1024]{1,0:T(8,128)(2,1)S(1)} %get-tuple-element.249), channel_id=1, source_target_pairs={{0,1},{1,0},{2,3},{3,2},{4,5},{5,4},{6,7},{7,6},{8,9},{9,8},{10,11... | collective-permute-start | bytes 3145736 | tf_op jit(solution)/shard_map/ppermute | solution.py:50
  161.1 13.0 %collective-permute-start.46 = (bf16[512,1024]{1,0:T(8,128)(2,1)S(1)}, bf16[512,1024]{1,0:T(8,128)(2,1)S(1)}, u32[]{:S(2)}, u32[]{:S(2)}) collective-permute-start(bf16[512,1024]{1,0:T(8,128)(2,1)S(1)} %get-tuple-element.250), channel_id=1, source_target_pairs={{0,1},{1,0},{2,3},{3,2},{4,5},{5,4},{6,7},{7,6},{8,9},{9,8},{10,11... | collective-permute-start | bytes 3145736 | tf_op jit(solution)/shard_map/ppermute | solution.py:50
  168.0 11.2 %collective-permute-start.42 = (bf16[3,8,8,1024]{3,2,1,0:T(8,128)(2,1)S(1)}, bf16[3,8,8,1024]{3,2,1,0:T(8,128)(2,1)S(1)}, u32[]{:S(2)}, u32[]{:S(2)}) collective-permute-start(bf16[3,8,8,1024]{3,2,1,0:T(8,128)(2,1)S(1)} %fusion.2), channel_id=1, source_target_pairs={{0,8},{1,25},{2,10},{3,27},{4,12},{5,29},{6,14},{7,31},{8,0},{9,17... | collective-permute-start | bytes 1179656 | tf_op jit(solution)/shard_map/ppermute | solution.py:46
  170.3 8.8 %collective-permute-start.43 = (bf16[3,8,8,1024]{3,2,1,0:T(8,128)(2,1)S(1)}, bf16[3,8,8,1024]{3,2,1,0:T(8,128)(2,1)S(1)}, u32[]{:S(2)}, u32[]{:S(2)}) collective-permute-start(bf16[3,8,8,1024]{3,2,1,0:T(8,128)(2,1)S(1)} %get-tuple-element.224), channel_id=1, source_target_pairs={{0,32},{1,97},{2,34},{3,99},{4,36},{5,101},{6,38},{7,103},{8,40},{... | collective-permute-start | bytes 1179656 | tf_op jit(solution)/shard_map/ppermute | solution.py:46
  173.6 7.8 %collective-permute-start.44 = (bf16[3,8,8,1024]{3,2,1,0:T(8,128)(2,1)S(1)}, bf16[3,8,8,1024]{3,2,1,0:T(8,128)(2,1)S(1)}, u32[]{:S(2)}, u32[]{:S(2)}) collective-permute-start(bf16[3,8,8,1024]{3,2,1,0:T(8,128)(2,1)S(1)} %get-tuple-element.225), channel_id=1, source_target_pairs={{0,2},{1,7},{2,0},{3,5},{4,6},{5,3},{6,4},{7,1},{8,10},{9,15},{10,... | collective-permute-start | bytes 1179656 | tf_op jit(solution)/shard_map/ppermute | solution.py:46
  191.4 4.8 %collective-permute-start.50 = (bf16[3,2,8,1024]{3,2,1,0:T(8,128)(2,1)S(1)}, bf16[3,2,8,1024]{3,2,1,0:T(8,128)(2,1)S(1)}, u32[]{:S(2)}, u32[]{:S(2)}) collective-permute-start(bf16[3,2,8,1024]{3,2,1,0:T(8,128)(2,1)S(1)} %fusion.7), channel_id=1, source_target_pairs={{0,2},{1,7},{2,0},{3,5},{4,6},{5,3},{6,4},{7,1},{8,10},{9,15},{10,... | collective-permute-start | bytes 294920 | tf_op jit(solution)/shard_map/ppermute | solution.py:46
  192.0 4.7 %collective-permute-start.51 = (bf16[3,2,8,1024]{3,2,1,0:T(8,128)(2,1)S(1)}, bf16[3,2,8,1024]{3,2,1,0:T(8,128)(2,1)S(1)}, u32[]{:S(2)}, u32[]{:S(2)}) collective-permute-start(bf16[3,2,8,1024]{3,2,1,0:T(8,128)(2,1)S(1)} %fusion.6), channel_id=1, source_target_pairs={{0,8},{1,25},{2,10},{3,27},{4,12},{5,29},{6,14},{7,31},{8,0},{9,17... | collective-permute-start | bytes 294920 | tf_op jit(solution)/shard_map/ppermute | solution.py:46
  (14 other events, 160.3 us)
where the time goes:
time: 203 us; the launch traced here: 199 us
  starting transfers between devices  84.2 us (41%)
  waiting for transfers between devices  64.9 us (32%)
  Pallas kernels  44.9 us (22%)
  other arithmetic  3.6 us (2%)
    ppermute x45, starting transfers between devices, hop(): return lax.ppermute(value, BOTH, step_pairs(axis, offsets))  71.1 us
    ppermute x45, waiting for transfers between devices, hop(): return lax.ppermute(value, BOTH, step_pairs(axis, offsets))  64.9 us
    ppermute x8, starting transfers between devices, swap(): return lax.ppermute(value, BOTH, CORE_PAIRS)  13.1 us
    pallas_call x3, Pallas kernels, first(): pl.pallas_call(first_kernel, out_shape=[jax.ShapeDtypeStruct((3, rows, 12...  12.2 us
    pallas_call x3, Pallas kernels, second(): pl.pallas_call(second_kernel, out_shape=[shape_of(2, 3, 32, columns)] * 4...  11.6 us
    pallas_call x2, Pallas kernels, rows_out(): pl.pallas_call(functools.partial(rows_kernel, start), out_shape=[shape_of...  8.16 us
    pallas_call x3, Pallas kernels, unweave(): pl.pallas_call(unweave_kernel, out_shape=[jax.ShapeDtypeStruct((3, 2, exp...  5.04 us
  transfers between devices with their start and end apart: 53, of which 26 were waited for; matrix products, arithmetic and copies ran while one was open for 1% of the time, Pallas kernels for 16%

commit v1 on v0

--- a/solution.py
+++ b/solution.py
@@ -141,9 +141,9 @@
     )(table, own, came, last)
 
 
-def pick_kernel(table_ref, p0, p1, p2, p3, *outs):
+def pick_kernel(table_ref, p0, p1, p2, p3, own, ahead, back):
     spot = spots(table_ref[8])
-    for index, out in enumerate(outs):
+    for index, out in enumerate((own, ahead.at[0], back, ahead.at[1])):
         for k in range(2):
             e = table_ref[2 * index + k]
             for b, p in enumerate((p0, p1, p2, p3)):
@@ -154,38 +154,32 @@
     columns = plane[0].shape[-1]
     return pl.pallas_call(
         pick_kernel,
-        out_shape=[shape_of(2, 3, 4, 8, columns)] * 4,
+        out_shape=[shape_of(*lead, 2, 3, 4, 8, columns) for lead in ((), (2,), ())],
         in_specs=[SMEM] + [VMEM] * 4,
-        out_specs=[VMEM] * 4,
+        out_specs=[VMEM] * 3,
         compiler_params=LIMIT,
         name="pick",
     )(table, *plane)
 
 
-def first_kernel(table_ref, tok0, tok1, cot0, cot1, mask, a0, a1, a2, a3, sums, weights):
+def first_kernel(table_ref, tok0, tok1, cot0, cot1, mask, own, came, back, across, sums, weights):
     core = table_ref[8]
-    columns = a0.shape[-1]
+    columns = own.shape[-1]
     rows = tok0.shape[0]
-    step = 256
-    for spot, a in zip(spots(core), (a0, a1, a2, a3)):
+    for spot, a in zip(spots(core), (own, came.at[0], back, across)):
         weights[:, :, spot] = a[...]
     half = pl.ds(pl.multiple_of(core * columns, columns), columns)
-    w = [
-        (weights[k, 0:2].reshape(256, columns), weights[k, 2].reshape(128, columns))
-        for k in range(2)
-    ]
-    for b, (tok, cot) in enumerate(((tok0, cot0), (tok1, cot1))):
-        for r in range(0, rows, step):
-            here = slice(r, r + step)
-            there = slice(rows * b + r, rows * b + r + step)
-            chosen = mask[there] > 0.0
-            tok_part = tok[here, half]
-            cot_part = cot[here, half]
-            pre = [contract_last(tok_part, w[k][0]) for k in range(2)]
-            d_hidden = [contract_last(cot_part, w[k][1]) for k in range(2)]
-            sums[0, there] = jnp.where(chosen, pre[0][:, :128], pre[1][:, :128])
-            sums[1, there] = jnp.where(chosen, pre[0][:, 128:], pre[1][:, 128:])
-            sums[2, there] = jnp.where(chosen, d_hidden[0], d_hidden[1])
+    w_pair = jnp.concatenate([weights[k, 0:2].reshape(256, columns) for k in range(2)], 0)
+    w_down = jnp.concatenate([weights[k, 2].reshape(128, columns) for k in range(2)], 0)
+    parts = ((tok0[:, half], cot0[:, half]), (tok1[...], cot1[...]))
+    for b, (tok, cot) in enumerate(parts):
+        here = slice(rows * b, rows * b + rows)
+        chosen = mask[here] > 0.0
+        pre = contract_last(tok, w_pair)
+        d_hidden = contract_last(cot, w_down)
+        sums[0, here] = jnp.where(chosen, pre[:, :128], pre[:, 256:384])
+        sums[1, here] = jnp.where(chosen, pre[:, 128:256], pre[:, 384:])
+        sums[2, here] = jnp.where(chosen, d_hidden[:, :128], d_hidden[:, 128:])
 
 
 def first(table, rows_in, mask, arrived):
@@ -205,10 +199,10 @@
 
 
 def second_kernel(
-    table_ref, tok0, tok1, cot0, cot1, mask, sums, got, o0, o1, o2, o3, hidden, pair, turned
+    table_ref, tok0, tok1, cot0, cot1, mask, sums, got, own, ahead, back, hidden, pair, turned
 ):
     core = table_ref[8]
-    columns = o0.shape[-1]
+    columns = own.shape[-1]
     rows = tok0.shape[0]
     step = 256
     for r in range(0, 2 * rows, step):
@@ -237,26 +231,31 @@
     for c in range(0, columns, step):
         cols = pl.ds(start + c, step)
         out_cols = slice(c, c + step)
-        both = matmul(turned[:512, :rows], tok0[:, cols]) + matmul(turned[:512, rows:], tok1[:, cols])
-        down = matmul(turned[512:, :rows], cot0[:, cols]) + matmul(turned[512:, rows:], cot1[:, cols])
+        both = matmul(turned[:512, :rows], tok0[:, cols]) + matmul(
+            turned[:512, rows:], tok1[:, out_cols]
+        )
+        down = matmul(turned[512:, :rows], cot0[:, cols]) + matmul(
+            turned[512:, rows:], cot1[:, out_cols]
+        )
         for k in range(2):
             for m in range(3):
                 line = both[256 * k + 128 * m :][:128] if m < 2 else down[128 * k :][:128]
                 line = line.astype(jnp.bfloat16)
                 q = [line[32 * i : 32 * i + 32] for i in range(4)]
-                o0[k, m, :, out_cols] = q[0]
-                o1[k, m, :, out_cols] = jnp.where(swapped, q[2], q[1])
-                o2[k, m, :, out_cols] = jnp.where(swapped, q[1], q[2])
-                o3[k, m, :, out_cols] = q[3]
+                own[k, m, :, out_cols] = q[0]
+                ahead[0, k, m, :, out_cols] = jnp.where(swapped, q[2], q[1])
+                back[k, m, :, out_cols] = jnp.where(swapped, q[1], q[2])
+                ahead[1, k, m, :, out_cols] = q[3]
 
 
 def second(table, rows_in, mask, sums, got, columns):
     rows = mask.shape[0]
     return pl.pallas_call(
         second_kernel,
-        out_shape=[shape_of(2, 3, 32, columns)] * 4 + [shape_of(rows, 256), shape_of(rows, 512)],
+        out_shape=[shape_of(*lead, 2, 3, 32, columns) for lead in ((), (2,), ())]
+        + [shape_of(rows, 256), shape_of(rows, 512)],
         in_specs=[SMEM] + [VMEM] * 7,
-        out_specs=[VMEM] * 6,
+        out_specs=[VMEM] * 5,
         scratch_shapes=[pltpu.VMEM((768, rows), jnp.bfloat16)],
         compiler_params=pltpu.CompilerParams(vmem_limit_bytes=24 * 1024 * 1024),
         name="second",
@@ -304,14 +303,14 @@
     )(table, *hidden, *pair, *weights, *added)
 
 
-def merge_kernel(table_ref, c0, c1, c2, c3, own, one, rest, total):
+def merge_kernel(table_ref, kept, came, back, across, own, one, rest, total):
     spot = spots(table_ref[8])
     total[...] = jnp.zeros_like(total)
-    for index, came in enumerate((c0, c1, c2, c3)):
+    for index, block in enumerate((kept, came.at[0], back, across)):
         for k in range(2):
             e = table_ref[2 * index + k]
             for p in range(4):
-                total[p, :, e] += came[k, :, p].astype(jnp.float32)
+                total[p, :, e] += block[k, :, p].astype(jnp.float32)
     own[...] = total[0].astype(jnp.bfloat16)
     one[...] = total[spot[1]].astype(jnp.bfloat16)
     rest[0] = total[spot[2]].astype(jnp.bfloat16)
@@ -328,7 +327,7 @@
         scratch_shapes=[pltpu.VMEM((4, 3, experts, 8, columns), jnp.float32)],
         compiler_params=LIMIT,
         name="merge",
-    )(table, *[c.reshape(2, 3, 4, 8, columns) for c in came])
+    )(table, *[c.reshape(*c.shape[:-2], 4, 8, columns) for c in came])
 
 
 def shards(tokens, cotangent, row_slot, placement, master, first_moment, second_moment):
@@ -355,7 +354,9 @@
     blocks = [narrow[:, 2 * c : 2 * c + 2] for c in each]
     (ones,) = together([hop(blocks[c], near[c], ONE) for c in each])
     rests = [hop(jnp.stack([blocks[c], ones[c]], 0), near[c], BACK) for c in each]
-    rows_in = [tokens, swap(tokens), cotangent, swap(cotangent)]
+    far = (1 - core) * columns
+    got_rows = [swap(lax.dynamic_slice_in_dim(v, far, columns, 1)) for v in (tokens, cotangent)]
+    rows_in = [tokens, got_rows[0], cotangent, got_rows[1]]
     slots = jnp.concatenate([row_slot, swap(row_slot)], 0)
     chosen = jnp.broadcast_to((slots == 0)[:, None], (2 * rows, 128)).astype(jnp.float32)
     rests, rows_in, chosen = together(rests, rows_in, chosen)
@@ -366,15 +367,21 @@
     backs, acrosses = together(backs, acrosses)
     packed = [pick(table[c], [lines[c], ones[c], backs[c], acrosses[c]]) for c in each]
     (packed,) = together(packed)
-    arrived = [
-        [packed[c][0]] + [hop(p, last[c], s) for p, s in zip(packed[c][1:], STEPS[1:])] for c in each
-    ]
-    (arrived,) = together(arrived)
+
+    def exchange(ahead, back, axis):
+        came = hop(ahead, axis, ONE)
+        return came, hop(back, axis, BACK), hop(came[1], axis, BACK)
+
+    (came,) = together([hop(packed[c][1], last[c], ONE) for c in each])
+    acrosses = [hop(came[c][1], last[c], BACK) for c in each]
+    backs = [hop(packed[c][2], last[c], BACK) for c in each]
+    backs, acrosses = together(backs, acrosses)
 
     sums = []
     weights = []
     for c in each:
-        blocks = [a.reshape(2, 3, 32, columns) for a in arrived[c]]
+        blocks = [packed[c][0], came[c], backs[c], acrosses[c]]
+        blocks = [a.reshape(*a.shape[:-3], 32, columns) for a in blocks]
         one_sums, one_weights = first(table[c], rows_in, chosen, blocks)
         sums.append(one_sums)
         weights.append(one_weights)
@@ -383,15 +390,13 @@
     hidden = []
     pair = []
     for c in each:
-        *packed, one_hidden, one_pair = second(table[c], rows_in, chosen, sums[c], got[c], columns)
-        sent.append(packed)
+        own, ahead, back, one_hidden, one_pair = second(
+            table[c], rows_in, chosen, sums[c], got[c], columns
+        )
+        sent.append((own, *exchange(ahead, back, last[c])))
         hidden.append(one_hidden)
         pair.append(one_pair)
-
-    merged = []
-    for c in each:
-        came = [sent[c][0]] + [hop(p, last[c], s) for p, s in zip(sent[c][1:], STEPS[1:])]
-        merged.append(merge(table[c], came, experts))
+    merged = [merge(table[c], sent[c], experts) for c in each]
 
     def add(one, came):
         return (one.astype(jnp.float32) + came[1].astype(jnp.float32)).astype(jnp.bfloat16)
@@ -399,8 +404,7 @@
     def scatter(parts, axes):
         (came,) = together([hop(parts[c][2], axes[c], BACK) for c in each])
         (ones,) = together([add(parts[c][1], came[c]) for c in each])
-        (ones,) = together([hop(ones[c], axes[c], ONE) for c in each])
-        return [(parts[c][0], came[c], ones[c]) for c in each]
+        return [(parts[c][0], came[c], hop(ones[c], axes[c], ONE)) for c in each]
 
     merged = scatter(merged, mid)
     sums = [unweave(table[c], *merged[c]) for c in each]

time: 203 us -> 204 us (level)
  the two profiles are of different devices: /device:TPU:1 before, /device:TPU:0 now
where the time goes in v1:
time: 204 us; the launch traced here: 200 us
  starting transfers between devices  74.5 us (37%)
  waiting for transfers between devices  71.1 us (35%)
  Pallas kernels  41.9 us (21%)
  other arithmetic  7.1 us (3%)
  local copies, waits for them, and re-layouts  4.55 us (2%)
    ppermute x45, waiting for transfers between devices, hop(): return lax.ppermute(value, BOTH, step_pairs(axis, offsets))  71.1 us
    ppermute x45, starting transfers between devices, hop(): return lax.ppermute(value, BOTH, step_pairs(axis, offsets))  68.6 us
    pallas_call x3, Pallas kernels, second(): pl.pallas_call(second_kernel, out_shape=[shape_of(*lead, 2, 3, 32, column...  10.6 us
    pallas_call x3, Pallas kernels, first(): pl.pallas_call(first_kernel, out_shape=[jax.ShapeDtypeStruct((3, rows, 12...  9.51 us
    pallas_call x2, Pallas kernels, rows_out(): pl.pallas_call(functools.partial(rows_kernel, start), out_shape=[shape_of...  8.16 us
    ppermute x8, starting transfers between devices, swap(): return lax.ppermute(value, BOTH, CORE_PAIRS)  5.95 us
    pallas_call x3, Pallas kernels, unweave(): pl.pallas_call(unweave_kernel, out_shape=[jax.ShapeDtypeStruct((3, 2, exp...  5.04 us
  transfers between devices with their start and end apart: 53, of which 26 were waited for; matrix products, arithmetic and copies ran while one was open for 4% of the time, Pallas kernels for 16%

profile of v1, /device:TPU:0, one launch (start us, length us, event | category | flops | bytes accessed | tf_op | source)
XLA Modules:
  0.0 200.4 jit_solution(9350427243093734127)
XLA Ops:
  2.5 2.0 collective-permute-start.2
  4.5 1.6 collective-permute-start.1
  7.6 2.3 %constant_dynamic-slice_fusion = bf16[512,1024]{1,0:T(8,128)(2,1)} fusion(bf16[512,2048]{1,0:T(8,128)(2,1)} %cot0.5, s32[]{:T(128)S(6)} %select_n.19), kind=kLoop, calls=%fused_computation.44 | loop fusion | bytes 2097156 | tf_op jit(solution)/shard_map/dynamic_slice | solution.py:358
  9.8 3.8 %collective-permute-start.7 = (bf16[512,1024]{1,0:T(8,128)(2,1)}, bf16[512,1024]{1,0:T(8,128)(2,1)S(1)}, u32[]{:S(2)}, u32[]{:S(2)}) collective-permute-start(bf16[512,1024]{1,0:T(8,128)(2,1)} %constant_dynamic-slice_fusion), channel_id=1, source_target_pairs={{0,1},{1,0},{2,3},{3,2},{4,5},{5,4},{6,7},{7,6},{8,9},{9,8},{10,11... | collective-permute-start | bytes 3145736 | tf_op jit(solution)/shard_map/ppermute | solution.py:50
  19.5 2.3 %collective-permute-start.5 = (bf16[2,3,2,8,1024]{4,3,2,1,0:T(8,128)(2,1)S(1)}, bf16[2,3,2,8,1024]{4,3,2,1,0:T(8,128)(2,1)S(1)}, u32[]{:S(2)}, u32[]{:S(2)}) collective-permute-start(bf16[2,3,2,8,1024]{4,3,2,1,0:T(8,128)(2,1)S(1)} %pad_maximum_fusion.3), channel_id=1, source_target_pairs={{0,96},{1,33},{2,98},{3,35},{4,100},{5,37},{6,102},{7,39},{8,104},... | collective-permute-start | bytes 589832 | tf_op jit(solution)/shard_map/ppermute | solution.py:46
  31.2 2.1 %collective-permute-start.12 = (bf16[3,8,8,1024]{3,2,1,0:T(8,128)(2,1)S(1)}, bf16[3,8,8,1024]{3,2,1,0:T(8,128)(2,1)S(1)}, u32[]{:S(2)}, u32[]{:S(2)}) collective-permute-start(bf16[3,8,8,1024]{3,2,1,0:T(8,128)(2,1)S(1)} %weave.3.p0), channel_id=1, source_target_pairs={{0,24},{1,9},{2,26},{3,11},{4,28},{5,13},{6,30},{7,15},{8,16},{9,1... | collective-permute-start | bytes 1179656 | tf_op jit(solution)/shard_map/ppermute | solution.py:46
  34.5 6.8 %collective-permute-done.9.p1 = bf16[3,8,8,1024]{3,2,1,0:T(8,128)(2,1)S(1)} collective-permute-done((bf16[3,8,8,1024]{3,2,1,0:T(8,128)(2,1)S(1)}, bf16[3,8,8,1024]{3,2,1,0:T(8,128)(2,1)S(1)}, u32[]{:S(2)}, u32[]{:S(2)}) %collective-permute-start.9) | collective-permute-done | bytes 393248 | tf_op jit(solution)/shard_map/ppermute | solution.py:46
  41.2 2.4 %collective-permute-start.14 = (bf16[3,8,8,1024]{3,2,1,0:T(8,128)(2,1)S(1)}, bf16[3,8,8,1024]{3,2,1,0:T(8,128)(2,1)S(1)}, u32[]{:S(2)}, u32[]{:S(2)}) collective-permute-start(bf16[3,8,8,1024]{3,2,1,0:T(8,128)(2,1)S(1)} %weave.5.p0), channel_id=1, source_target_pairs={{0,6},{1,3},{2,4},{3,1},{4,2},{5,7},{6,0},{7,5},{8,14},{9,11},{10,... | collective-permute-start | bytes 1179656 | tf_op jit(solution)/shard_map/ppermute | solution.py:46
  43.7 1.8 collective-permute-start.15
  45.4 2.4 %collective-permute-start.16 = (bf16[3,8,8,1024]{3,2,1,0:T(8,128)(2,1)S(1)}, bf16[3,8,8,1024]{3,2,1,0:T(8,128)(2,1)S(1)}, u32[]{:S(2)}, u32[]{:S(2)}) collective-permute-start(bf16[3,8,8,1024]{3,2,1,0:T(8,128)(2,1)S(1)} %collective-permute-done.10.p1), channel_id=1, source_target_pairs={{0,96},{1,33},{2,98},{3,35},{4,100},{5,37},{6,102},{7,39},{8,104},... | collective-permute-start | bytes 1179656 | tf_op jit(solution)/shard_map/ppermute | solution.py:46
  48.4 1.8 collective-permute-done.14.p2
  50.2 2.4 %collective-permute-done.15.p3 = bf16[3,8,8,1024]{3,2,1,0:T(8,128)(2,1)S(1)} collective-permute-done((bf16[3,8,8,1024]{3,2,1,0:T(8,128)(2,1)S(1)}, bf16[3,8,8,1024]{3,2,1,0:T(8,128)(2,1)S(1)}, u32[]{:S(2)}, u32[]{:S(2)}) %collective-permute-start.15) | collective-permute-done | bytes 393248 | tf_op jit(solution)/shard_map/ppermute | solution.py:46
  52.6 1.8 collective-permute-done.16.p3
  54.4 3.9 %collective-permute-done.17.p3 = bf16[3,8,8,1024]{3,2,1,0:T(8,128)(2,1)S(1)} collective-permute-done((bf16[3,8,8,1024]{3,2,1,0:T(8,128)(2,1)S(1)}, bf16[3,8,8,1024]{3,2,1,0:T(8,128)(2,1)S(1)}, u32[]{:S(2)}, u32[]{:S(2)}) %collective-permute-start.17) | collective-permute-done | bytes 393248 | tf_op jit(solution)/shard_map/ppermute | solution.py:46
  60.6 2.7 %collective-permute-start.21 = (bf16[2,3,4,8,1024]{4,3,2,1,0:T(8,128)(2,1)S(1)}, bf16[2,3,4,8,1024]{4,3,2,1,0:T(8,128)(2,1)S(1)}, u32[]{:S(2)}, u32[]{:S(2)}) collective-permute-start(bf16[2,3,4,8,1024]{4,3,2,1,0:T(8,128)(2,1)S(1)} %get-tuple-element.158), channel_id=1, source_target_pairs={{0,96},{1,33},{2,98},{3,35},{4,100},{5,37},{6,102},{7,39},{8,104},... | collective-permute-start | bytes 1179656 | tf_op jit(solution)/shard_map/ppermute | solution.py:46
  63.3 1.8 collective-permute-start.22
  65.1 11.6 %collective-permute-done.18 = bf16[2,2,3,4,8,1024]{5,4,3,2,1,0:T(8,128)(2,1)S(1)} collective-permute-done((bf16[2,2,3,4,8,1024]{5,4,3,2,1,0:T(8,128)(2,1)S(1)}, bf16[2,2,3,4,8,1024]{5,4,3,2,1,0:T(8,128)(2,1)S(1)}, u32[]{:S(2)}, u32[]{:S(2)}) %collective-permute-start.18) | collective-permute-done | bytes 786464 | tf_op jit(solution)/shard_map/ppermute | solution.py:46
  76.9 2.6 %collective-permute-done.20 = bf16[2,2,3,4,8,1024]{5,4,3,2,1,0:T(8,128)(2,1)S(1)} collective-permute-done((bf16[2,2,3,4,8,1024]{5,4,3,2,1,0:T(8,128)(2,1)S(1)}, bf16[2,2,3,4,8,1024]{5,4,3,2,1,0:T(8,128)(2,1)S(1)}, u32[]{:S(2)}, u32[]{:S(2)}) %collective-permute-start.20) | collective-permute-done | bytes 786464 | tf_op jit(solution)/shard_map/ppermute | solution.py:46
  80.9 4.5 %collective-permute-start.24 = (bf16[2,3,4,8,1024]{4,3,2,1,0:T(8,128)(2,1)S(1)}, bf16[2,3,4,8,1024]{4,3,2,1,0:T(8,128)(2,1)S(1)}, u32[]{:S(2)}, u32[]{:S(2)}) collective-permute-start(bf16[2,3,4,8,1024]{4,3,2,1,0:T(8,128)(2,1)S(1)} %slice_bitcast_fusion.5), channel_id=1, source_target_pairs={{0,96},{1,33},{2,98},{3,35},{4,100},{5,37},{6,102},{7,39},{8,104},... | collective-permute-start | bytes 1179656 | tf_op jit(solution)/shard_map/ppermute | solution.py:46
  85.6 4.2 %collective-permute-done.26 = bf16[2,3,4,8,1024]{4,3,2,1,0:T(8,128)(2,1)S(1)} collective-permute-done((bf16[2,3,4,8,1024]{4,3,2,1,0:T(8,128)(2,1)S(1)}, bf16[2,3,4,8,1024]{4,3,2,1,0:T(8,128)(2,1)S(1)}, u32[]{:S(2)}, u32[]{:S(2)}) %collective-permute-start.26) | collective-permute-done | bytes 393248 | tf_op jit(solution)/shard_map/ppermute | solution.py:46
  91.1 3.2 %first.3 = (f32[3,1024,128]{2,1,0:T(8,128)S(1)}, bf16[2,3,4,32,1024]{4,3,2,1,0:T(8,128)(2,1)S(1)}) custom-call(s32[9]{0:T(128)S(1)} %get-tuple-element.248.table_ref, bf16[512,2048]{1,0:T(8,128)(2,1)S(1)} %copy-done, bf16[512,1024]{1,0:T(8,128)(2,1)} %collective-permute-done.6.tok1, bf16[512,2048]{1,0:T(8,128)(2,1)S(1)} %copy-done.1, ...), custom_call_target="tpu_custom_call" | custom-call | tf_op jit(solution)/shard_map/first/pallas_call | solution.py:188
  94.6 3.2 %first.4 = (f32[3,1024,128]{2,1,0:T(8,128)S(1)}, bf16[2,3,4,32,1024]{4,3,2,1,0:T(8,128)(2,1)S(1)}) custom-call(s32[9]{0:T(128)S(1)} %get-tuple-element.247.table_ref, bf16[512,2048]{1,0:T(8,128)(2,1)S(1)} %copy-done, bf16[512,1024]{1,0:T(8,128)(2,1)} %collective-permute-done.6.tok1, bf16[512,2048]{1,0:T(8,128)(2,1)S(1)} %copy-done.1, ...), custom_call_target="tpu_custom_call" | custom-call | tf_op jit(solution)/shard_map/first/pallas_call | solution.py:188
  98.4 3.2 %first.5 = (f32[3,1024,128]{2,1,0:T(8,128)S(1)}, bf16[2,3,4,32,1024]{4,3,2,1,0:T(8,128)(2,1)S(1)}) custom-call(s32[9]{0:T(128)S(1)} %get-tuple-element.246.table_ref, bf16[512,2048]{1,0:T(8,128)(2,1)S(1)} %copy-done, bf16[512,1024]{1,0:T(8,128)(2,1)} %collective-permute-done.6.tok1, bf16[512,2048]{1,0:T(8,128)(2,1)S(1)} %copy-done.1, ...), custom_call_target="tpu_custom_call" | custom-call | tf_op jit(solution)/shard_map/first/pallas_call | solution.py:188
  101.7 3.5 %second.3 = (bf16[2,3,32,1024]{3,2,1,0:T(8,128)(2,1)S(1)}, bf16[2,2,3,32,1024]{4,3,2,1,0:T(8,128)(2,1)S(1)}, bf16[2,3,32,1024]{3,2,1,0:T(8,128)(2,1)S(1)}, bf16[...) custom-call(s32[9]{0:T(128)S(1)} %get-tuple-element.248.table_ref, bf16[512,2048]{1,0:T(8,128)(2,1)S(1)} %copy-done, ...), custom_call_target="tpu_custom_call" | custom-call | tf_op jit(solution)/shard_map/second/pallas_call | solution.py:253
  105.2 1.8 collective-permute-start.28
  107.0 3.5 %second.4 = (bf16[2,3,32,1024]{3,2,1,0:T(8,128)(2,1)S(1)}, bf16[2,2,3,32,1024]{4,3,2,1,0:T(8,128)(2,1)S(1)}, bf16[2,3,32,1024]{3,2,1,0:T(8,128)(2,1)S(1)}, bf16[...) custom-call(s32[9]{0:T(128)S(1)} %get-tuple-element.247.table_ref, bf16[512,2048]{1,0:T(8,128)(2,1)S(1)} %copy-done, ...), custom_call_target="tpu_custom_call" | custom-call | tf_op jit(solution)/shard_map/second/pallas_call | solution.py:253
  111.9 3.5 %second.5 = (bf16[2,3,32,1024]{3,2,1,0:T(8,128)(2,1)S(1)}, bf16[2,2,3,32,1024]{4,3,2,1,0:T(8,128)(2,1)S(1)}, bf16[2,3,32,1024]{3,2,1,0:T(8,128)(2,1)S(1)}, bf16[...) custom-call(s32[9]{0:T(128)S(1)} %get-tuple-element.246.table_ref, bf16[512,2048]{1,0:T(8,128)(2,1)S(1)} %copy-done, ...), custom_call_target="tpu_custom_call" | custom-call | tf_op jit(solution)/shard_map/second/pallas_call | solution.py:253
  116.8 1.6 collective-permute-start.34
  118.4 2.5 %collective-permute-start.39 = (bf16[2,3,32,1024]{3,2,1,0:T(8,128)(2,1)S(1)}, bf16[2,3,32,1024]{3,2,1,0:T(8,128)(2,1)S(1)}, u32[]{:S(2)}, u32[]{:S(2)}) collective-permute-start(bf16[2,3,32,1024]{3,2,1,0:T(8,128)(2,1)S(1)} %get-tuple-element.185), channel_id=1, source_target_pairs={{0,24},{1,9},{2,26},{3,11},{4,28},{5,13},{6,30},{7,15},{8,16},{9,1... | collective-permute-start | bytes 1179656 | tf_op jit(solution)/shard_map/ppermute | solution.py:46
  121.0 2.8 %collective-permute-done.33 = bf16[2,2,3,32,1024]{4,3,2,1,0:T(8,128)(2,1)S(1)} collective-permute-done((bf16[2,2,3,32,1024]{4,3,2,1,0:T(8,128)(2,1)S(1)}, bf16[2,2,3,32,1024]{4,3,2,1,0:T(8,128)(2,1)S(1)}, u32[]{:S(2)}, u32[]{:S(2)}) %collective-permute-start.33) | collective-permute-done | bytes 786464 | tf_op jit(solution)/shard_map/ppermute | solution.py:46
  123.7 1.7 collective-permute-start.30
  125.5 6.2 %collective-permute-done.38 = bf16[2,2,3,32,1024]{4,3,2,1,0:T(8,128)(2,1)S(1)} collective-permute-done((bf16[2,2,3,32,1024]{4,3,2,1,0:T(8,128)(2,1)S(1)}, bf16[2,2,3,32,1024]{4,3,2,1,0:T(8,128)(2,1)S(1)}, u32[]{:S(2)}, u32[]{:S(2)}) %collective-permute-start.38) | collective-permute-done | bytes 786464 | tf_op jit(solution)/shard_map/ppermute | solution.py:46
  133.1 12.0 %collective-permute-start.40 = (bf16[2,3,32,1024]{3,2,1,0:T(8,128)(2,1)S(1)}, bf16[2,3,32,1024]{3,2,1,0:T(8,128)(2,1)S(1)}, u32[]{:S(2)}, u32[]{:S(2)}) collective-permute-start(bf16[2,3,32,1024]{3,2,1,0:T(8,128)(2,1)S(1)} %slice_bitcast_fusion), channel_id=1, source_target_pairs={{0,24},{1,9},{2,26},{3,11},{4,28},{5,13},{6,30},{7,15},{8,16},{9,1... | collective-permute-start | bytes 1179656 | tf_op jit(solution)/shard_map/ppermute | solution.py:46
  148.7 3.1 %collective-permute-done.40 = bf16[2,3,32,1024]{3,2,1,0:T(8,128)(2,1)S(1)} collective-permute-done((bf16[2,3,32,1024]{3,2,1,0:T(8,128)(2,1)S(1)}, bf16[2,3,32,1024]{3,2,1,0:T(8,128)(2,1)S(1)}, u32[]{:S(2)}, u32[]{:S(2)}) %collective-permute-start.40) | collective-permute-done | bytes 393248 | tf_op jit(solution)/shard_map/ppermute | solution.py:46
  152.9 2.0 collective-permute-start.41
  154.9 3.1 %rows_out.2 = (bf16[512,1024]{1,0:T(8,128)(2,1)S(1)}, bf16[512,1024]{1,0:T(8,128)(2,1)S(1)}) custom-call(s32[9]{0:T(128)S(1)} %get-tuple-element.248.table_ref, bf16[1024,256]{1,0:T(8,128)(2,1)S(1)} %get-tuple-element.207.refs_0_, bf16[1024,256]{1,0:T(8,128)(2,1)S(1)} %get-tuple-element.208.refs_1_, bf16[1024,256]{1,0:T(8,128)(2,1)S(1)} %get-tuple-element.209.refs_2_, ...), custom_call_target="tpu_custom_call" | custom-call | tf_op jit(solution)/shard_map/rows_out/pallas_call | solution.py:296
  161.7 4.5 %collective-permute-done.41.came = bf16[2,3,8,8,1024]{4,3,2,1,0:T(8,128)(2,1)S(1)} collective-permute-done((bf16[2,3,8,8,1024]{4,3,2,1,0:T(8,128)(2,1)S(1)}, bf16[2,3,8,8,1024]{4,3,2,1,0:T(8,128)(2,1)S(1)}, u32[]{:S(2)}, u32[]{:S(2)}) %collective-permute-start.41) | collective-permute-done | bytes 786464 | tf_op jit(solution)/shard_map/ppermute | solution.py:46
  166.8 2.1 %collective-permute-start.43 = (bf16[3,8,8,1024]{3,2,1,0:T(8,128)(2,1)S(1)}, bf16[3,8,8,1024]{3,2,1,0:T(8,128)(2,1)S(1)}, u32[]{:S(2)}, u32[]{:S(2)}) collective-permute-start(bf16[3,8,8,1024]{3,2,1,0:T(8,128)(2,1)S(1)} %get-tuple-element.198), channel_id=1, source_target_pairs={{0,32},{1,97},{2,34},{3,99},{4,36},{5,101},{6,38},{7,103},{8,40},{... | collective-permute-start | bytes 1179656 | tf_op jit(solution)/shard_map/ppermute | solution.py:46
  168.8 5.0 %rows_out.3 = (bf16[512,2048]{1,0:T(8,128)(2,1)}, bf16[512,2048]{1,0:T(8,128)(2,1)}) custom-call(s32[9]{0:T(128)S(1)} %get-tuple-element.248.table_ref, bf16[1024,256]{1,0:T(8,128)(2,1)S(1)} %get-tuple-element.207.refs_0_, bf16[1024,256]{1,0:T(8,128)(2,1)S(1)} %get-tuple-element.208.refs_1_, bf16[1024,256]{1,0:T(8,128)(2,1)S(1)} %get-tuple-element.209.refs_2_, ...), custom_call_target="tpu_custom_call" | custom-call | tf_op jit(solution)/shard_map/rows_out/pallas_call | solution.py:296
  174.5 1.7 unweave.3
  176.2 1.7 unweave.4
  177.9 1.7 unweave.5
  179.6 2.0 collective-permute-start.47
  181.6 2.2 %collective-permute-start.48 = (bf16[2,3,2,8,1024]{4,3,2,1,0:T(8,128)(2,1)S(1)}, bf16[2,3,2,8,1024]{4,3,2,1,0:T(8,128)(2,1)S(1)}, u32[]{:S(2)}, u32[]{:S(2)}) collective-permute-start(bf16[2,3,2,8,1024]{4,3,2,1,0:T(8,128)(2,1)S(1)} %get-tuple-element.224), channel_id=1, source_target_pairs={{0,24},{1,9},{2,26},{3,11},{4,28},{5,13},{6,30},{7,15},{8,16},{9,1... | collective-permute-start | bytes 589832 | tf_op jit(solution)/shard_map/ppermute | solution.py:46
  186.6 1.9 collective-permute-done.48
  188.5 2.5 %collective-permute-done.49 = bf16[2,3,2,8,1024]{4,3,2,1,0:T(8,128)(2,1)S(1)} collective-permute-done((bf16[2,3,2,8,1024]{4,3,2,1,0:T(8,128)(2,1)S(1)}, bf16[2,3,2,8,1024]{4,3,2,1,0:T(8,128)(2,1)S(1)}, u32[]{:S(2)}, u32[]{:S(2)}) %collective-permute-start.49) | collective-permute-done | bytes 196640 | tf_op jit(solution)/shard_map/ppermute | solution.py:46
  191.0 1.7 collective-permute-start.50
  194.0 1.7 collective-permute-done.50
  (123 shorter events, 49.0 us)
Async XLA Ops:
  2.5 12.7 %collective-permute-start.2 = (bf16[3,2,8,1024]{3,2,1,0:T(8,128)(2,1)S(1)}, bf16[3,2,8,1024]{3,2,1,0:T(8,128)(2,1)S(1)}, u32[]{:S(2)}, u32[]{:S(2)}) collective-permute-start(bf16[3,2,8,1024]{3,2,1,0:T(8,128)(2,1)S(1)} %get-tuple-element.243.own), channel_id=1, source_target_pairs={{0,32},{1,97},{2,34},{3,99},{4,36},{5,101},{6,38},{7,103},{8,40},{... | collective-permute-start | bytes 294920 | tf_op jit(solution)/shard_map/ppermute | solution.py:46
  4.5 11.2 %collective-permute-start.1 = (bf16[3,2,8,1024]{3,2,1,0:T(8,128)(2,1)S(1)}, bf16[3,2,8,1024]{3,2,1,0:T(8,128)(2,1)}, u32[]{:S(2)}, u32[]{:S(2)}) collective-permute-start(bf16[3,2,8,1024]{3,2,1,0:T(8,128)(2,1)S(1)} %get-tuple-element.244.own), channel_id=1, source_target_pairs={{0,8},{1,25},{2,10},{3,27},{4,12},{5,29},{6,14},{7,31},{8,0},{9,17... | collective-permute-start | bytes 294920 | tf_op jit(solution)/shard_map/ppermute | solution.py:46
  6.1 9.7 %collective-permute-start = (bf16[3,2,8,1024]{3,2,1,0:T(8,128)(2,1)S(1)}, bf16[3,2,8,1024]{3,2,1,0:T(8,128)(2,1)}, u32[]{:S(2)}, u32[]{:S(2)}) collective-permute-start(bf16[3,2,8,1024]{3,2,1,0:T(8,128)(2,1)S(1)} %get-tuple-element.245.own), channel_id=1, source_target_pairs={{0,2},{1,7},{2,0},{3,5},{4,6},{5,3},{6,4},{7,1},{8,10},{9,15},{10,... | collective-permute-start | bytes 294920 | tf_op jit(solution)/shard_map/ppermute | solution.py:46
  9.8 16.6 %collective-permute-start.7 = (bf16[512,1024]{1,0:T(8,128)(2,1)}, bf16[512,1024]{1,0:T(8,128)(2,1)S(1)}, u32[]{:S(2)}, u32[]{:S(2)}) collective-permute-start(bf16[512,1024]{1,0:T(8,128)(2,1)} %constant_dynamic-slice_fusion), channel_id=1, source_target_pairs={{0,1},{1,0},{2,3},{3,2},{4,5},{5,4},{6,7},{7,6},{8,9},{9,8},{10,11... | collective-permute-start | bytes 3145736 | tf_op jit(solution)/shard_map/ppermute | solution.py:50
  14.7 11.7 %collective-permute-start.6 = (bf16[512,1024]{1,0:T(8,128)(2,1)}, bf16[512,1024]{1,0:T(8,128)(2,1)}, u32[]{:S(2)}, u32[]{:S(2)}) collective-permute-start(bf16[512,1024]{1,0:T(8,128)(2,1)} %constant_dynamic-slice_fusion.1), channel_id=1, source_target_pairs={{0,1},{1,0},{2,3},{3,2},{4,5},{5,4},{6,7},{7,6},{8,9},{9,8},{10,11... | collective-permute-start | bytes 3145736 | tf_op jit(solution)/shard_map/ppermute | solution.py:50
  16.7 7.0 %collective-permute-start.3 = (bf16[2,3,2,8,1024]{4,3,2,1,0:T(8,128)(2,1)S(1)}, bf16[2,3,2,8,1024]{4,3,2,1,0:T(8,128)(2,1)S(1)}, u32[]{:S(2)}, u32[]{:S(2)}) collective-permute-start(bf16[2,3,2,8,1024]{4,3,2,1,0:T(8,128)(2,1)S(1)} %pad_maximum_fusion.1), channel_id=1, source_target_pairs={{0,6},{1,3},{2,4},{3,1},{4,2},{5,7},{6,0},{7,5},{8,14},{9,11},{10,... | collective-permute-start | bytes 589832 | tf_op jit(solution)/shard_map/ppermute | solution.py:46
  18.2 7.0 %collective-permute-start.4 = (bf16[2,3,2,8,1024]{4,3,2,1,0:T(8,128)(2,1)S(1)}, bf16[2,3,2,8,1024]{4,3,2,1,0:T(8,128)(2,1)S(1)}, u32[]{:S(2)}, u32[]{:S(2)}) collective-permute-start(bf16[2,3,2,8,1024]{4,3,2,1,0:T(8,128)(2,1)S(1)} %pad_maximum_fusion.2), channel_id=1, source_target_pairs={{0,24},{1,9},{2,26},{3,11},{4,28},{5,13},{6,30},{7,15},{8,16},{9,1... | collective-permute-start | bytes 589832 | tf_op jit(solution)/shard_map/ppermute | solution.py:46
  19.5 7.0 %collective-permute-start.5 = (bf16[2,3,2,8,1024]{4,3,2,1,0:T(8,128)(2,1)S(1)}, bf16[2,3,2,8,1024]{4,3,2,1,0:T(8,128)(2,1)S(1)}, u32[]{:S(2)}, u32[]{:S(2)}) collective-permute-start(bf16[2,3,2,8,1024]{4,3,2,1,0:T(8,128)(2,1)S(1)} %pad_maximum_fusion.3), channel_id=1, source_target_pairs={{0,96},{1,33},{2,98},{3,35},{4,100},{5,37},{6,102},{7,39},{8,104},... | collective-permute-start | bytes 589832 | tf_op jit(solution)/shard_map/ppermute | solution.py:46
  29.8 11.4 %collective-permute-start.9 = (bf16[3,8,8,1024]{3,2,1,0:T(8,128)(2,1)S(1)}, bf16[3,8,8,1024]{3,2,1,0:T(8,128)(2,1)S(1)}, u32[]{:S(2)}, u32[]{:S(2)}) collective-permute-start(bf16[3,8,8,1024]{3,2,1,0:T(8,128)(2,1)S(1)} %weave.3.p0), channel_id=1, source_target_pairs={{0,8},{1,25},{2,10},{3,27},{4,12},{5,29},{6,14},{7,31},{8,0},{9,17... | collective-permute-start | bytes 1179656 | tf_op jit(solution)/shard_map/ppermute | solution.py:46
  30.3 13.3 %collective-permute-start.10 = (bf16[3,8,8,1024]{3,2,1,0:T(8,128)(2,1)S(1)}, bf16[3,8,8,1024]{3,2,1,0:T(8,128)(2,1)S(1)}, u32[]{:S(2)}, u32[]{:S(2)}) collective-permute-start(bf16[3,8,8,1024]{3,2,1,0:T(8,128)(2,1)S(1)} %weave.4.p0), channel_id=1, source_target_pairs={{0,32},{1,97},{2,34},{3,99},{4,36},{5,101},{6,38},{7,103},{8,40},{... | collective-permute-start | bytes 1179656 | tf_op jit(solution)/shard_map/ppermute | solution.py:46
  30.6 13.0 %collective-permute-start.11 = (bf16[3,8,8,1024]{3,2,1,0:T(8,128)(2,1)S(1)}, bf16[3,8,8,1024]{3,2,1,0:T(8,128)(2,1)S(1)}, u32[]{:S(2)}, u32[]{:S(2)}) collective-permute-start(bf16[3,8,8,1024]{3,2,1,0:T(8,128)(2,1)S(1)} %weave.5.p0), channel_id=1, source_target_pairs={{0,2},{1,7},{2,0},{3,5},{4,6},{5,3},{6,4},{7,1},{8,10},{9,15},{10,... | collective-permute-start | bytes 1179656 | tf_op jit(solution)/shard_map/ppermute | solution.py:46
  31.2 16.7 %collective-permute-start.12 = (bf16[3,8,8,1024]{3,2,1,0:T(8,128)(2,1)S(1)}, bf16[3,8,8,1024]{3,2,1,0:T(8,128)(2,1)S(1)}, u32[]{:S(2)}, u32[]{:S(2)}) collective-permute-start(bf16[3,8,8,1024]{3,2,1,0:T(8,128)(2,1)S(1)} %weave.3.p0), channel_id=1, source_target_pairs={{0,24},{1,9},{2,26},{3,11},{4,28},{5,13},{6,30},{7,15},{8,16},{9,1... | collective-permute-start | bytes 1179656 | tf_op jit(solution)/shard_map/ppermute | solution.py:46
  33.3 15.1 %collective-permute-start.13 = (bf16[3,8,8,1024]{3,2,1,0:T(8,128)(2,1)S(1)}, bf16[3,8,8,1024]{3,2,1,0:T(8,128)(2,1)S(1)}, u32[]{:S(2)}, u32[]{:S(2)}) collective-permute-start(bf16[3,8,8,1024]{3,2,1,0:T(8,128)(2,1)S(1)} %weave.4.p0), channel_id=1, source_target_pairs={{0,96},{1,33},{2,98},{3,35},{4,100},{5,37},{6,102},{7,39},{8,104},... | collective-permute-start | bytes 1179656 | tf_op jit(solution)/shard_map/ppermute | solution.py:46
  41.2 9.0 %collective-permute-start.14 = (bf16[3,8,8,1024]{3,2,1,0:T(8,128)(2,1)S(1)}, bf16[3,8,8,1024]{3,2,1,0:T(8,128)(2,1)S(1)}, u32[]{:S(2)}, u32[]{:S(2)}) collective-permute-start(bf16[3,8,8,1024]{3,2,1,0:T(8,128)(2,1)S(1)} %weave.5.p0), channel_id=1, source_target_pairs={{0,6},{1,3},{2,4},{3,1},{4,2},{5,7},{6,0},{7,5},{8,14},{9,11},{10,... | collective-permute-start | bytes 1179656 | tf_op jit(solution)/shard_map/ppermute | solution.py:46
  43.7 9.0 %collective-permute-start.15 = (bf16[3,8,8,1024]{3,2,1,0:T(8,128)(2,1)S(1)}, bf16[3,8,8,1024]{3,2,1,0:T(8,128)(2,1)S(1)}, u32[]{:S(2)}, u32[]{:S(2)}) collective-permute-start(bf16[3,8,8,1024]{3,2,1,0:T(8,128)(2,1)S(1)} %collective-permute-done.9.p1), channel_id=1, source_target_pairs={{0,24},{1,9},{2,26},{3,11},{4,28},{5,13},{6,30},{7,15},{8,16},{9,1... | collective-permute-start | bytes 1179656 | tf_op jit(solution)/shard_map/ppermute | solution.py:46
  45.4 9.0 %collective-permute-start.16 = (bf16[3,8,8,1024]{3,2,1,0:T(8,128)(2,1)S(1)}, bf16[3,8,8,1024]{3,2,1,0:T(8,128)(2,1)S(1)}, u32[]{:S(2)}, u32[]{:S(2)}) collective-permute-start(bf16[3,8,8,1024]{3,2,1,0:T(8,128)(2,1)S(1)} %collective-permute-done.10.p1), channel_id=1, source_target_pairs={{0,96},{1,33},{2,98},{3,35},{4,100},{5,37},{6,102},{7,39},{8,104},... | collective-permute-start | bytes 1179656 | tf_op jit(solution)/shard_map/ppermute | solution.py:46
  47.9 10.5 %collective-permute-start.17 = (bf16[3,8,8,1024]{3,2,1,0:T(8,128)(2,1)S(1)}, bf16[3,8,8,1024]{3,2,1,0:T(8,128)(2,1)S(1)}, u32[]{:S(2)}, u32[]{:S(2)}) collective-permute-start(bf16[3,8,8,1024]{3,2,1,0:T(8,128)(2,1)S(1)} %collective-permute-done.11.p1), channel_id=1, source_target_pairs={{0,6},{1,3},{2,4},{3,1},{4,2},{5,7},{6,0},{7,5},{8,14},{9,11},{10,... | collective-permute-start | bytes 1179656 | tf_op jit(solution)/shard_map/ppermute | solution.py:46
  60.4 16.3 %collective-permute-start.18 = (bf16[2,2,3,4,8,1024]{5,4,3,2,1,0:T(8,128)(2,1)S(1)}, bf16[2,2,3,4,8,1024]{5,4,3,2,1,0:T(8,128)(2,1)S(1)}, u32[]{:S(2)}, u32[]{:S(2)}) collective-permute-start(bf16[2,2,3,4,8,1024]{5,4,3,2,1,0:T(8,128)(2,1)S(1)} %get-tuple-element.154), channel_id=1, source_target_pairs={{0,32},{1,97},{2,34},{3,99},{4,36},{5,101},{6,38},{7,103},{8,40},{... | collective-permute-start | bytes 2359304 | tf_op jit(solution)/shard_map/ppermute | solution.py:46
  60.5 16.5 %collective-permute-start.19 = (bf16[2,2,3,4,8,1024]{5,4,3,2,1,0:T(8,128)(2,1)S(1)}, bf16[2,2,3,4,8,1024]{5,4,3,2,1,0:T(8,128)(2,1)S(1)}, u32[]{:S(2)}, u32[]{:S(2)}) collective-permute-start(bf16[2,2,3,4,8,1024]{5,4,3,2,1,0:T(8,128)(2,1)S(1)} %get-tuple-element.155), channel_id=1, source_target_pairs={{0,2},{1,7},{2,0},{3,5},{4,6},{5,3},{6,4},{7,1},{8,10},{9,15},{10,... | collective-permute-start | bytes 2359304 | tf_op jit(solution)/shard_map/ppermute | solution.py:46
  60.5 19.0 %collective-permute-start.20 = (bf16[2,2,3,4,8,1024]{5,4,3,2,1,0:T(8,128)(2,1)S(1)}, bf16[2,2,3,4,8,1024]{5,4,3,2,1,0:T(8,128)(2,1)S(1)}, u32[]{:S(2)}, u32[]{:S(2)}) collective-permute-start(bf16[2,2,3,4,8,1024]{5,4,3,2,1,0:T(8,128)(2,1)S(1)} %get-tuple-element.156), channel_id=1, source_target_pairs={{0,8},{1,25},{2,10},{3,27},{4,12},{5,29},{6,14},{7,31},{8,0},{9,17... | collective-permute-start | bytes 2359304 | tf_op jit(solution)/shard_map/ppermute | solution.py:46
  60.6 20.2 %collective-permute-start.21 = (bf16[2,3,4,8,1024]{4,3,2,1,0:T(8,128)(2,1)S(1)}, bf16[2,3,4,8,1024]{4,3,2,1,0:T(8,128)(2,1)S(1)}, u32[]{:S(2)}, u32[]{:S(2)}) collective-permute-start(bf16[2,3,4,8,1024]{4,3,2,1,0:T(8,128)(2,1)S(1)} %get-tuple-element.158), channel_id=1, source_target_pairs={{0,96},{1,33},{2,98},{3,35},{4,100},{5,37},{6,102},{7,39},{8,104},... | collective-permute-start | bytes 1179656 | tf_op jit(solution)/shard_map/ppermute | solution.py:46
  63.3 22.0 %collective-permute-start.22 = (bf16[2,3,4,8,1024]{4,3,2,1,0:T(8,128)(2,1)S(1)}, bf16[2,3,4,8,1024]{4,3,2,1,0:T(8,128)(2,1)S(1)}, u32[]{:S(2)}, u32[]{:S(2)}) collective-permute-start(bf16[2,3,4,8,1024]{4,3,2,1,0:T(8,128)(2,1)S(1)} %get-tuple-element.159), channel_id=1, source_target_pairs={{0,6},{1,3},{2,4},{3,1},{4,2},{5,7},{6,0},{7,5},{8,14},{9,11},{10,... | collective-permute-start | bytes 1179656 | tf_op jit(solution)/shard_map/ppermute | solution.py:46
  76.6 9.0 %collective-permute-start.23 = (bf16[2,3,4,8,1024]{4,3,2,1,0:T(8,128)(2,1)S(1)}, bf16[2,3,4,8,1024]{4,3,2,1,0:T(8,128)(2,1)S(1)}, u32[]{:S(2)}, u32[]{:S(2)}) collective-permute-start(bf16[2,3,4,8,1024]{4,3,2,1,0:T(8,128)(2,1)S(1)} %get-tuple-element.160), channel_id=1, source_target_pairs={{0,24},{1,9},{2,26},{3,11},{4,28},{5,13},{6,30},{7,15},{8,16},{9,1... | collective-permute-start | bytes 1179656 | tf_op jit(solution)/shard_map/ppermute | solution.py:46
  79.6 10.2 %collective-permute-start.26 = (bf16[2,3,4,8,1024]{4,3,2,1,0:T(8,128)(2,1)S(1)}, bf16[2,3,4,8,1024]{4,3,2,1,0:T(8,128)(2,1)S(1)}, u32[]{:S(2)}, u32[]{:S(2)}) collective-permute-start(bf16[2,3,4,8,1024]{4,3,2,1,0:T(8,128)(2,1)S(1)} %slice_bitcast_fusion.3), channel_id=1, source_target_pairs={{0,24},{1,9},{2,26},{3,11},{4,28},{5,13},{6,30},{7,15},{8,16},{9,1... | collective-permute-start | bytes 1179656 | tf_op jit(solution)/shard_map/ppermute | solution.py:46
  80.8 9.0 %collective-permute-start.25 = (bf16[2,3,4,8,1024]{4,3,2,1,0:T(8,128)(2,1)S(1)}, bf16[2,3,4,8,1024]{4,3,2,1,0:T(8,128)(2,1)S(1)}, u32[]{:S(2)}, u32[]{:S(2)}) collective-permute-start(bf16[2,3,4,8,1024]{4,3,2,1,0:T(8,128)(2,1)S(1)} %slice_bitcast_fusion.4), channel_id=1, source_target_pairs={{0,6},{1,3},{2,4},{3,1},{4,2},{5,7},{6,0},{7,5},{8,14},{9,11},{10,... | collective-permute-start | bytes 1179656 | tf_op jit(solution)/shard_map/ppermute | solution.py:46
  80.9 10.2 %collective-permute-start.24 = (bf16[2,3,4,8,1024]{4,3,2,1,0:T(8,128)(2,1)S(1)}, bf16[2,3,4,8,1024]{4,3,2,1,0:T(8,128)(2,1)S(1)}, u32[]{:S(2)}, u32[]{:S(2)}) collective-permute-start(bf16[2,3,4,8,1024]{4,3,2,1,0:T(8,128)(2,1)S(1)} %slice_bitcast_fusion.5), channel_id=1, source_target_pairs={{0,96},{1,33},{2,98},{3,35},{4,100},{5,37},{6,102},{7,39},{8,104},... | collective-permute-start | bytes 1179656 | tf_op jit(solution)/shard_map/ppermute | solution.py:46
  94.3 7.4 %collective-permute-start.27 = (f32[3,1024,128]{2,1,0:T(8,128)S(1)}, f32[3,1024,128]{2,1,0:T(8,128)S(1)}, u32[]{:S(2)}, u32[]{:S(2)}) collective-permute-start(f32[3,1024,128]{2,1,0:T(8,128)S(1)} %get-tuple-element.165.sums), channel_id=1, source_target_pairs={{0,1},{1,0},{2,3},{3,2},{4,5},{5,4},{6,7},{7,6},{8,9},{9,8},{10,11... | collective-permute-start | bytes 4718600 | tf_op jit(solution)/shard_map/ppermute | solution.py:50
  97.8 9.2 %collective-permute-start.32 = (f32[3,1024,128]{2,1,0:T(8,128)S(1)}, f32[3,1024,128]{2,1,0:T(8,128)S(1)}, u32[]{:S(2)}, u32[]{:S(2)}) collective-permute-start(f32[3,1024,128]{2,1,0:T(8,128)S(1)} %get-tuple-element.174.sums), channel_id=1, source_target_pairs={{0,1},{1,0},{2,3},{3,2},{4,5},{5,4},{6,7},{7,6},{8,9},{9,8},{10,11... | collective-permute-start | bytes 4718600 | tf_op jit(solution)/shard_map/ppermute | solution.py:50
  101.6 10.3 %collective-permute-start.37 = (f32[3,1024,128]{2,1,0:T(8,128)S(1)}, f32[3,1024,128]{2,1,0:T(8,128)S(1)}, u32[]{:S(2)}, u32[]{:S(2)}) collective-permute-start(f32[3,1024,128]{2,1,0:T(8,128)S(1)} %get-tuple-element.182.sums), channel_id=1, source_target_pairs={{0,1},{1,0},{2,3},{3,2},{4,5},{5,4},{6,7},{7,6},{8,9},{9,8},{10,11... | collective-permute-start | bytes 4718600 | tf_op jit(solution)/shard_map/ppermute | solution.py:50
  105.2 13.2 %collective-permute-start.28 = (bf16[2,2,3,32,1024]{4,3,2,1,0:T(8,128)(2,1)S(1)}, bf16[2,2,3,32,1024]{4,3,2,1,0:T(8,128)(2,1)S(1)}, u32[]{:S(2)}, u32[]{:S(2)}) collective-permute-start(bf16[2,2,3,32,1024]{4,3,2,1,0:T(8,128)(2,1)S(1)} %get-tuple-element.167), channel_id=1, source_target_pairs={{0,32},{1,97},{2,34},{3,99},{4,36},{5,101},{6,38},{7,103},{8,40},{... | collective-permute-start | bytes 2359304 | tf_op jit(solution)/shard_map/ppermute | solution.py:46
  110.5 13.2 %collective-permute-start.33 = (bf16[2,2,3,32,1024]{4,3,2,1,0:T(8,128)(2,1)S(1)}, bf16[2,2,3,32,1024]{4,3,2,1,0:T(8,128)(2,1)S(1)}, u32[]{:S(2)}, u32[]{:S(2)}) collective-permute-start(bf16[2,2,3,32,1024]{4,3,2,1,0:T(8,128)(2,1)S(1)} %get-tuple-element.176), channel_id=1, source_target_pairs={{0,2},{1,7},{2,0},{3,5},{4,6},{5,3},{6,4},{7,1},{8,10},{9,15},{10,... | collective-permute-start | bytes 2359304 | tf_op jit(solution)/shard_map/ppermute | solution.py:46
  115.4 16.3 %collective-permute-start.38 = (bf16[2,2,3,32,1024]{4,3,2,1,0:T(8,128)(2,1)S(1)}, bf16[2,2,3,32,1024]{4,3,2,1,0:T(8,128)(2,1)S(1)}, u32[]{:S(2)}, u32[]{:S(2)}) collective-permute-start(bf16[2,2,3,32,1024]{4,3,2,1,0:T(8,128)(2,1)S(1)} %get-tuple-element.184), channel_id=1, source_target_pairs={{0,8},{1,25},{2,10},{3,27},{4,12},{5,29},{6,14},{7,31},{8,0},{9,17... | collective-permute-start | bytes 2359304 | tf_op jit(solution)/shard_map/ppermute | solution.py:46
  115.5 17.6 %collective-permute-start.29 = (bf16[2,3,32,1024]{3,2,1,0:T(8,128)(2,1)S(1)}, bf16[2,3,32,1024]{3,2,1,0:T(8,128)(2,1)S(1)}, u32[]{:S(2)}, u32[]{:S(2)}) collective-permute-start(bf16[2,3,32,1024]{3,2,1,0:T(8,128)(2,1)S(1)} %get-tuple-element.168), channel_id=1, source_target_pairs={{0,96},{1,33},{2,98},{3,35},{4,100},{5,37},{6,102},{7,39},{8,104},... | collective-permute-start | bytes 1179656 | tf_op jit(solution)/shard_map/ppermute | solution.py:46
  116.8 30.4 %collective-permute-start.34 = (bf16[2,3,32,1024]{3,2,1,0:T(8,128)(2,1)S(1)}, bf16[2,3,32,1024]{3,2,1,0:T(8,128)(2,1)S(1)}, u32[]{:S(2)}, u32[]{:S(2)}) collective-permute-start(bf16[2,3,32,1024]{3,2,1,0:T(8,128)(2,1)S(1)} %get-tuple-element.177), channel_id=1, source_target_pairs={{0,6},{1,3},{2,4},{3,1},{4,2},{5,7},{6,0},{7,5},{8,14},{9,11},{10,... | collective-permute-start | bytes 1179656 | tf_op jit(solution)/shard_map/ppermute | solution.py:46
  118.4 30.3 %collective-permute-start.39 = (bf16[2,3,32,1024]{3,2,1,0:T(8,128)(2,1)S(1)}, bf16[2,3,32,1024]{3,2,1,0:T(8,128)(2,1)S(1)}, u32[]{:S(2)}, u32[]{:S(2)}) collective-permute-start(bf16[2,3,32,1024]{3,2,1,0:T(8,128)(2,1)S(1)} %get-tuple-element.185), channel_id=1, source_target_pairs={{0,24},{1,9},{2,26},{3,11},{4,28},{5,13},{6,30},{7,15},{8,16},{9,1... | collective-permute-start | bytes 1179656 | tf_op jit(solution)/shard_map/ppermute | solution.py:46
  123.7 21.3 %collective-permute-start.30 = (bf16[2,3,32,1024]{3,2,1,0:T(8,128)(2,1)S(1)}, bf16[2,3,32,1024]{3,2,1,0:T(8,128)(2,1)S(1)}, u32[]{:S(2)}, u32[]{:S(2)}) collective-permute-start(bf16[2,3,32,1024]{3,2,1,0:T(8,128)(2,1)S(1)} %slice_bitcast_fusion.2), channel_id=1, source_target_pairs={{0,96},{1,33},{2,98},{3,35},{4,100},{5,37},{6,102},{7,39},{8,104},... | collective-permute-start | bytes 1179656 | tf_op jit(solution)/shard_map/ppermute | solution.py:46
  131.7 15.6 %collective-permute-start.35 = (bf16[2,3,32,1024]{3,2,1,0:T(8,128)(2,1)S(1)}, bf16[2,3,32,1024]{3,2,1,0:T(8,128)(2,1)S(1)}, u32[]{:S(2)}, u32[]{:S(2)}) collective-permute-start(bf16[2,3,32,1024]{3,2,1,0:T(8,128)(2,1)S(1)} %slice_bitcast_fusion.1), channel_id=1, source_target_pairs={{0,6},{1,3},{2,4},{3,1},{4,2},{5,7},{6,0},{7,5},{8,14},{9,11},{10,... | collective-permute-start | bytes 1179656 | tf_op jit(solution)/shard_map/ppermute | solution.py:46
  133.1 18.7 %collective-permute-start.40 = (bf16[2,3,32,1024]{3,2,1,0:T(8,128)(2,1)S(1)}, bf16[2,3,32,1024]{3,2,1,0:T(8,128)(2,1)S(1)}, u32[]{:S(2)}, u32[]{:S(2)}) collective-permute-start(bf16[2,3,32,1024]{3,2,1,0:T(8,128)(2,1)S(1)} %slice_bitcast_fusion), channel_id=1, source_target_pairs={{0,24},{1,9},{2,26},{3,11},{4,28},{5,13},{6,30},{7,15},{8,16},{9,1... | collective-permute-start | bytes 1179656 | tf_op jit(solution)/shard_map/ppermute | solution.py:46
  146.2 13.9 %collective-permute-start.31 = (bf16[2,3,8,8,1024]{4,3,2,1,0:T(8,128)(2,1)S(1)}, bf16[2,3,8,8,1024]{4,3,2,1,0:T(8,128)(2,1)S(1)}, u32[]{:S(2)}, u32[]{:S(2)}) collective-permute-start(bf16[2,3,8,8,1024]{4,3,2,1,0:T(8,128)(2,1)S(1)} %get-tuple-element.170), channel_id=1, source_target_pairs={{0,24},{1,9},{2,26},{3,11},{4,28},{5,13},{6,30},{7,15},{8,16},{9,1... | collective-permute-start | bytes 2359304 | tf_op jit(solution)/shard_map/ppermute | solution.py:46
  148.4 13.3 %collective-permute-start.36 = (bf16[2,3,8,8,1024]{4,3,2,1,0:T(8,128)(2,1)S(1)}, bf16[2,3,8,8,1024]{4,3,2,1,0:T(8,128)(2,1)S(1)}, u32[]{:S(2)}, u32[]{:S(2)}) collective-permute-start(bf16[2,3,8,8,1024]{4,3,2,1,0:T(8,128)(2,1)S(1)} %get-tuple-element.178), channel_id=1, source_target_pairs={{0,96},{1,33},{2,98},{3,35},{4,100},{5,37},{6,102},{7,39},{8,104},... | collective-permute-start | bytes 2359304 | tf_op jit(solution)/shard_map/ppermute | solution.py:46
  152.9 13.3 %collective-permute-start.41 = (bf16[2,3,8,8,1024]{4,3,2,1,0:T(8,128)(2,1)S(1)}, bf16[2,3,8,8,1024]{4,3,2,1,0:T(8,128)(2,1)S(1)}, u32[]{:S(2)}, u32[]{:S(2)}) collective-permute-start(bf16[2,3,8,8,1024]{4,3,2,1,0:T(8,128)(2,1)S(1)} %get-tuple-element.186), channel_id=1, source_target_pairs={{0,6},{1,3},{2,4},{3,1},{4,2},{5,7},{6,0},{7,5},{8,14},{9,11},{10,... | collective-permute-start | bytes 2359304 | tf_op jit(solution)/shard_map/ppermute | solution.py:46
  158.0 10.8 %collective-permute-start.45 = (bf16[512,1024]{1,0:T(8,128)(2,1)S(1)}, bf16[512,1024]{1,0:T(8,128)(2,1)S(1)}, u32[]{:S(2)}, u32[]{:S(2)}) collective-permute-start(bf16[512,1024]{1,0:T(8,128)(2,1)S(1)} %get-tuple-element.216), channel_id=1, source_target_pairs={{0,1},{1,0},{2,3},{3,2},{4,5},{5,4},{6,7},{7,6},{8,9},{9,8},{10,11... | collective-permute-start | bytes 3145736 | tf_op jit(solution)/shard_map/ppermute | solution.py:50
  158.1 10.7 %collective-permute-start.46 = (bf16[512,1024]{1,0:T(8,128)(2,1)S(1)}, bf16[512,1024]{1,0:T(8,128)(2,1)S(1)}, u32[]{:S(2)}, u32[]{:S(2)}) collective-permute-start(bf16[512,1024]{1,0:T(8,128)(2,1)S(1)} %get-tuple-element.217), channel_id=1, source_target_pairs={{0,1},{1,0},{2,3},{3,2},{4,5},{5,4},{6,7},{7,6},{8,9},{9,8},{10,11... | collective-permute-start | bytes 3145736 | tf_op jit(solution)/shard_map/ppermute | solution.py:50
  166.7 7.9 %collective-permute-start.42 = (bf16[3,8,8,1024]{3,2,1,0:T(8,128)(2,1)S(1)}, bf16[3,8,8,1024]{3,2,1,0:T(8,128)(2,1)S(1)}, u32[]{:S(2)}, u32[]{:S(2)}) collective-permute-start(bf16[3,8,8,1024]{3,2,1,0:T(8,128)(2,1)S(1)} %fusion.2), channel_id=1, source_target_pairs={{0,8},{1,25},{2,10},{3,27},{4,12},{5,29},{6,14},{7,31},{8,0},{9,17... | collective-permute-start | bytes 1179656 | tf_op jit(solution)/shard_map/ppermute | solution.py:46
  166.8 9.5 %collective-permute-start.43 = (bf16[3,8,8,1024]{3,2,1,0:T(8,128)(2,1)S(1)}, bf16[3,8,8,1024]{3,2,1,0:T(8,128)(2,1)S(1)}, u32[]{:S(2)}, u32[]{:S(2)}) collective-permute-start(bf16[3,8,8,1024]{3,2,1,0:T(8,128)(2,1)S(1)} %get-tuple-element.198), channel_id=1, source_target_pairs={{0,32},{1,97},{2,34},{3,99},{4,36},{5,101},{6,38},{7,103},{8,40},{... | collective-permute-start | bytes 1179656 | tf_op jit(solution)/shard_map/ppermute | solution.py:46
  168.8 9.1 %collective-permute-start.44 = (bf16[3,8,8,1024]{3,2,1,0:T(8,128)(2,1)S(1)}, bf16[3,8,8,1024]{3,2,1,0:T(8,128)(2,1)S(1)}, u32[]{:S(2)}, u32[]{:S(2)}) collective-permute-start(bf16[3,8,8,1024]{3,2,1,0:T(8,128)(2,1)S(1)} %get-tuple-element.203), channel_id=1, source_target_pairs={{0,2},{1,7},{2,0},{3,5},{4,6},{5,3},{6,4},{7,1},{8,10},{9,15},{10,... | collective-permute-start | bytes 1179656 | tf_op jit(solution)/shard_map/ppermute | solution.py:46
  179.6 7.0 %collective-permute-start.47 = (bf16[2,3,2,8,1024]{4,3,2,1,0:T(8,128)(2,1)S(1)}, bf16[2,3,2,8,1024]{4,3,2,1,0:T(8,128)(2,1)S(1)}, u32[]{:S(2)}, u32[]{:S(2)}) collective-permute-start(bf16[2,3,2,8,1024]{4,3,2,1,0:T(8,128)(2,1)S(1)} %get-tuple-element.223), channel_id=1, source_target_pairs={{0,6},{1,3},{2,4},{3,1},{4,2},{5,7},{6,0},{7,5},{8,14},{9,11},{10,... | collective-permute-start | bytes 589832 | tf_op jit(solution)/shard_map/ppermute | solution.py:46
  183.8 7.2 %collective-permute-start.49 = (bf16[2,3,2,8,1024]{4,3,2,1,0:T(8,128)(2,1)S(1)}, bf16[2,3,2,8,1024]{4,3,2,1,0:T(8,128)(2,1)S(1)}, u32[]{:S(2)}, u32[]{:S(2)}) collective-permute-start(bf16[2,3,2,8,1024]{4,3,2,1,0:T(8,128)(2,1)S(1)} %get-tuple-element.225), channel_id=1, source_target_pairs={{0,96},{1,33},{2,98},{3,35},{4,100},{5,37},{6,102},{7,39},{8,104},... | collective-permute-start | bytes 589832 | tf_op jit(solution)/shard_map/ppermute | solution.py:46
  (13 other events, 139.9 us)
